TPU v7x, 768 devices: a whole 4x8x12 slice. The times are simulated.
768 devices in a mesh: row: 48 (over x, z_lo, core), col: 16 (over y, z_hi).
Axes of the slice: x: 4, y: 8, z: 12 (z_hi: 2, z_lo: 6; z = z_hi * 6 + z_lo), core: 2. Of those that a mesh axis runs over, the one named last changes fastest.
Arguments:
- picture_embeds: bfloat16 [196608, 1152], P(('row', 'col')), may hold values from -6 to 6
- caption_embeds: bfloat16 [196608, 1152], P(('row', 'col')), may hold values from -6 to 6
- logit_multiplier: float32 [1], replicated, may hold values from 5 to 20
- offset_shift: float32 [1], replicated, may hold values from -3 to -1
Outputs:
- d_images: float32 [196608, 1152], P(('row', 'col'))
- d_texts: float32 [196608, 1152], P(('row', 'col'))
All inputs are finite; a program needn't handle non-finite values.
Results may differ from a plain program's by a relative error of at most 0.0044.
Values may be sent and summed in bfloat16 or wider, within the bound.
No kernel may reach another device: no remote copies, remote signals or barrier semaphores. Data moves between devices by JAX's collectives and lax.ppermute only.
A program may use at most 32 MiB of HBM per device.

v0:
```python
import jax
import jax.numpy as jnp
from jax import lax
from jax.sharding import PartitionSpec as P

BLOCK_COUPLES = 256


def from_behind(block, axis, distance):
    devices = range(lax.axis_size(axis))
    route = [((i - distance) % len(devices), i) for i in devices]
    return lax.ppermute(block, axis, route)


def normalize(block):
    values = block.astype(jnp.float32)
    norm = jnp.sqrt(jnp.sum(values * values, axis=-1, keepdims=True) + 1e-06)
    return (values / norm, norm)


def block_coefficient_array(
    normed_picture_rows, normed_caption_rows, logit_multiplier, offset_shift, target_signs
):
    cosine_grid = lax.dot_general(
        normed_picture_rows,
        normed_caption_rows,
        (((1,), (1,)), ((), ())),
        preferred_element_type=jnp.float32,
    )
    similarity_raw = logit_multiplier[0] * cosine_grid + offset_shift[0]
    sigmoid_outputs = jax.nn.sigmoid(similarity_raw)
    if target_signs:
        sigmoid_outputs = sigmoid_outputs - jnp.eye(BLOCK_COUPLES, dtype=jnp.float32)
    return (sigmoid_outputs * (logit_multiplier[0] / BLOCK_COUPLES)).astype(jnp.bfloat16)


def forward_use(weights, normed_caption_rows):
    return jnp.dot(weights, normed_caption_rows, preferred_element_type=jnp.float32)


def backward_use(weights, normed_picture_rows):
    return lax.dot_general(
        weights, normed_picture_rows, (((0,), (0,)), ((), ())), preferred_element_type=jnp.float32
    )


def project_back(grad_unit, unit_float, norm):
    inner = jnp.sum(unit_float * grad_unit, axis=-1, keepdims=True)
    return (grad_unit - unit_float * inner) / norm


def per_device(picture_embeds, caption_embeds, logit_multiplier, offset_shift):
    image_float, image_norm = normalize(picture_embeds)
    normed_picture_rows = image_float.astype(jnp.bfloat16)
    text_float, text_norm = normalize(caption_embeds)
    normed_caption_rows = text_float.astype(jnp.bfloat16)
    earlier_normed_caption = from_behind(normed_caption_rows, "row", 1)
    own_normed_caption = from_behind(earlier_normed_caption, "col", 1)
    leading_summand = block_coefficient_array(
        normed_picture_rows, normed_caption_rows, logit_multiplier, offset_shift, True
    )
    middle_summand = block_coefficient_array(
        normed_picture_rows, earlier_normed_caption, logit_multiplier, offset_shift, False
    )
    trailing_summand = block_coefficient_array(
        normed_picture_rows, own_normed_caption, logit_multiplier, offset_shift, False
    )
    d_image_unit = (
        forward_use(leading_summand, normed_caption_rows)
        + forward_use(middle_summand, earlier_normed_caption)
        + forward_use(trailing_summand, own_normed_caption)
    )
    own_text = backward_use(leading_summand, normed_picture_rows)
    term_prev = backward_use(middle_summand, normed_picture_rows)
    term_diag = backward_use(trailing_summand, normed_picture_rows)
    returned = from_behind(term_diag, "col", -1)
    combined = term_prev + returned
    home_terms = from_behind(combined, "row", -1)
    d_text_unit = own_text + home_terms
    d_images = project_back(d_image_unit, image_float, image_norm)
    d_texts = project_back(d_text_unit, text_float, text_norm)
    return (d_images, d_texts)


def solution(mesh):
    placed = (P(("row", "col"), None), P(("row", "col"), None), P(), P())
    return jax.shard_map(
        per_device,
        mesh=mesh,
        in_specs=placed,
        out_specs=(P(("row", "col"), None), P(("row", "col"), None)),
        check_vma=False,
    )
```

profile of v0, /device:TPU:1, one launch (start us, length us, event | category | flops | bytes accessed | tf_op | source)
XLA Modules:
  0.0 171.4 jit_solution(17188767412316051097)
XLA Ops:
  0.6 1.3 fusion.1
  2.0 1.3 fusion.25
  3.3 5.4 %collective-permute-start = (bf16[256,1152]{1,0:T(8,128)(2,1)S(1)}, bf16[256,1152]{1,0:T(8,128)(2,1)S(1)}, u32[]{:S(2)}, u32[]{:S(2)}) collective-permute-start(bf16[256,1152]{1,0:T(8,128)(2,1)S(1)} %fusion.25), channel_id=1, source_target_pairs={{752,0},{0,16},{16,32},{32,48},{48,64},{64,80},{80,96},{96,112},{1... | collective-permute-start | bytes 1769480 | tf_op jit(solution)/shard_map/ppermute | solution.py:12
  8.7 0.2 fusion
  8.9 8.3 %collective-permute-done = bf16[256,1152]{1,0:T(8,128)(2,1)S(1)} collective-permute-done((bf16[256,1152]{1,0:T(8,128)(2,1)S(1)}, bf16[256,1152]{1,0:T(8,128)(2,1)S(1)}, u32[]{:S(2)}, u32[]{:S(2)}) %collective-permute-start) | collective-permute-done | bytes 589856 | tf_op jit(solution)/shard_map/ppermute | solution.py:12
  17.2 12.8 %collective-permute-start.1 = (bf16[256,1152]{1,0:T(8,128)(2,1)S(1)}, bf16[256,1152]{1,0:T(8,128)(2,1)S(1)}, u32[]{:S(2)}, u32[]{:S(2)}) collective-permute-start(bf16[256,1152]{1,0:T(8,128)(2,1)S(1)} %collective-permute-done), channel_id=1, source_target_pairs={{15,0},{0,1},{1,2},{2,3},{3,4},{4,5},{5,6},{6,7},{7,8},{8,9},{9,10... | collective-permute-start | bytes 1769480 | tf_op jit(solution)/shard_map/ppermute | solution.py:12
  31.3 0.2 fusion.24
  31.6 8.8 %collective-permute-done.1 = bf16[256,1152]{1,0:T(8,128)(2,1)S(1)} collective-permute-done((bf16[256,1152]{1,0:T(8,128)(2,1)S(1)}, bf16[256,1152]{1,0:T(8,128)(2,1)S(1)}, u32[]{:S(2)}, u32[]{:S(2)}) %collective-permute-start.1) | collective-permute-done | bytes 589856 | tf_op jit(solution)/shard_map/ppermute | solution.py:12
  40.4 0.4 fusion.23
  40.8 0.4 fusion.28
  41.2 9.6 %collective-permute-start.2 = (f32[256,1152]{1,0:T(8,128)S(1)}, f32[256,1152]{1,0:T(8,128)S(1)}, u32[]{:S(2)}, u32[]{:S(2)}) collective-permute-start(f32[256,1152]{1,0:T(8,128)S(1)} %fusion.28), channel_id=1, source_target_pairs={{1,0},{2,1},{3,2},{4,3},{5,4},{6,5},{7,6},{8,7},{9,8},{10,9},{11,1... | collective-permute-start | bytes 3538952 | tf_op jit(solution)/shard_map/ppermute | solution.py:12
  50.8 0.4 fusion.21
  51.2 0.4 fusion.27
  51.6 0.3 fusion.26
  51.9 0.4 fusion.22
  52.3 40.9 %collective-permute-done.2 = f32[256,1152]{1,0:T(8,128)S(1)} collective-permute-done((f32[256,1152]{1,0:T(8,128)S(1)}, f32[256,1152]{1,0:T(8,128)S(1)}, u32[]{:S(2)}, u32[]{:S(2)}) %collective-permute-start.2) | collective-permute-done | bytes 1179680 | tf_op jit(solution)/shard_map/ppermute | solution.py:12
  93.2 0.4 convolution_add_fusion
  93.6 12.7 %collective-permute-start.3 = (f32[256,1152]{1,0:T(8,128)S(1)}, f32[256,1152]{1,0:T(8,128)S(1)}, u32[]{:S(2)}, u32[]{:S(2)}) collective-permute-start(f32[256,1152]{1,0:T(8,128)S(1)} %convolution_add_fusion), channel_id=1, source_target_pairs={{16,0},{32,16},{48,32},{64,48},{80,64},{96,80},{112,96},{128,112},... | collective-permute-start | bytes 3538952 | tf_op jit(solution)/shard_map/ppermute | solution.py:12
  106.3 0.3 convolution_add_fusion.2
  106.6 0.5 multiply_reduce_fusion.1
  107.1 1.3 subtract_divide_fusion.1
  108.4 61.4 %collective-permute-done.3 = f32[256,1152]{1,0:T(8,128)S(1)} collective-permute-done((f32[256,1152]{1,0:T(8,128)S(1)}, f32[256,1152]{1,0:T(8,128)S(1)}, u32[]{:S(2)}, u32[]{:S(2)}) %collective-permute-start.3) | collective-permute-done | bytes 1179680 | tf_op jit(solution)/shard_map/ppermute | solution.py:12
  169.8 0.3 multiply_reduce_fusion
  170.1 1.3 subtract_divide_fusion
  (6 shorter events, 0.0 us)
Async XLA Ops:
  0.6 8.0 %copy-start.1 = (bf16[256,1152]{1,0:T(8,128)(2,1)S(1)}, bf16[256,1152]{1,0:T(8,128)(2,1)}, u32[]{:S(2)}) copy-start(bf16[256,1152]{1,0:T(8,128)(2,1)} %param.4) | copy-start | bytes 1769476
  3.3 13.9 %collective-permute-start = (bf16[256,1152]{1,0:T(8,128)(2,1)S(1)}, bf16[256,1152]{1,0:T(8,128)(2,1)S(1)}, u32[]{:S(2)}, u32[]{:S(2)}) collective-permute-start(bf16[256,1152]{1,0:T(8,128)(2,1)S(1)} %fusion.25), channel_id=1, source_target_pairs={{752,0},{0,16},{16,32},{32,48},{48,64},{64,80},{80,96},{96,112},{1... | collective-permute-start | bytes 1769480 | tf_op jit(solution)/shard_map/ppermute | solution.py:12
  17.2 23.2 %collective-permute-start.1 = (bf16[256,1152]{1,0:T(8,128)(2,1)S(1)}, bf16[256,1152]{1,0:T(8,128)(2,1)S(1)}, u32[]{:S(2)}, u32[]{:S(2)}) collective-permute-start(bf16[256,1152]{1,0:T(8,128)(2,1)S(1)} %collective-permute-done), channel_id=1, source_target_pairs={{15,0},{0,1},{1,2},{2,3},{3,4},{4,5},{5,6},{6,7},{7,8},{8,9},{9,10... | collective-permute-start | bytes 1769480 | tf_op jit(solution)/shard_map/ppermute | solution.py:12
  41.2 52.0 %collective-permute-start.2 = (f32[256,1152]{1,0:T(8,128)S(1)}, f32[256,1152]{1,0:T(8,128)S(1)}, u32[]{:S(2)}, u32[]{:S(2)}) collective-permute-start(f32[256,1152]{1,0:T(8,128)S(1)} %fusion.28), channel_id=1, source_target_pairs={{1,0},{2,1},{3,2},{4,3},{5,4},{6,5},{7,6},{8,7},{9,8},{10,9},{11,1... | collective-permute-start | bytes 3538952 | tf_op jit(solution)/shard_map/ppermute | solution.py:12
  93.6 76.2 %collective-permute-start.3 = (f32[256,1152]{1,0:T(8,128)S(1)}, f32[256,1152]{1,0:T(8,128)S(1)}, u32[]{:S(2)}, u32[]{:S(2)}) collective-permute-start(f32[256,1152]{1,0:T(8,128)S(1)} %convolution_add_fusion), channel_id=1, source_target_pairs={{16,0},{32,16},{48,32},{64,48},{80,64},{96,80},{112,96},{128,112},... | collective-permute-start | bytes 3538952 | tf_op jit(solution)/shard_map/ppermute | solution.py:12
  107.1 62.7 %copy-start = (bf16[256,1152]{1,0:T(8,128)(2,1)S(1)}, bf16[256,1152]{1,0:T(8,128)(2,1)}, u32[]{:S(2)}) copy-start(bf16[256,1152]{1,0:T(8,128)(2,1)} %param.5) | copy-start | bytes 1769476
where the time goes:
time: 173 us; the launch traced here: 171 us
  waiting for transfers between devices  119 us (69%)
  starting transfers between devices  40.5 us (23%)
  other arithmetic  5.96 us (3%)
  matrix products  3.47 us (2%)
  between operations  2.05 us (1%)
    ppermute x4, waiting for transfers between devices, from_behind(): return lax.ppermute(block, axis, route)  119 us
    ppermute x4, starting transfers between devices, from_behind(): return lax.ppermute(block, axis, route)  40.5 us
  transfers between devices with their start and end apart: 4, of which 4 were waited for; matrix products, arithmetic and copies ran while one was open for 2% of the time, Pallas kernels for 0%

commit v1 on v0

v1 whole, which is shorter than its diff:
```python
import jax
import jax.numpy as jnp
from jax import lax
from jax.sharding import PartitionSpec as P

BLOCK_COUPLES = 256
AXES = ("row", "col")


def moved(block, rows_on, cols_on):
    n_row, n_col = (lax.axis_size(a) for a in AXES)
    route = [
        (r * n_col + c, (r + rows_on) % n_row * n_col + (c + cols_on) % n_col)
        for r in range(n_row)
        for c in range(n_col)
    ]
    return lax.ppermute(block, AXES, route)


def normalize(block):
    values = block.astype(jnp.float32)
    norm = jnp.sqrt(jnp.sum(values * values, axis=-1, keepdims=True) + 1e-06)
    return (values / norm, norm)


def unit(block):
    return normalize(block)[0].astype(jnp.bfloat16)


def weights_of(left, right, logit_multiplier, offset_shift, matched):
    cosine = lax.dot_general(
        left, right, (((1,), (1,)), ((), ())), preferred_element_type=jnp.float32
    )
    share = jax.nn.sigmoid(logit_multiplier[0] * cosine + offset_shift[0])
    if matched:
        share = share - jnp.eye(BLOCK_COUPLES, dtype=jnp.float32)
    return (share * (logit_multiplier[0] / BLOCK_COUPLES)).astype(jnp.bfloat16)


def project_back(grad_unit, unit_float, norm):
    inner = jnp.sum(unit_float * grad_unit, axis=-1, keepdims=True)
    return (grad_unit - unit_float * inner) / norm


def per_device(picture_embeds, caption_embeds, logit_multiplier, offset_shift):
    text_diag = moved(caption_embeds, 1, 1)
    image_diag = moved(picture_embeds, -1, -1)
    text_before = moved(caption_embeds, 1, 0)
    image_after = moved(picture_embeds, -1, 0)

    def side(own, others, other_own, matched):
        grad = None
        own_unit = unit(own)
        for k, other in enumerate([other_own, *others]):
            other_unit = unit(other)
            weights = weights_of(own_unit, other_unit, logit_multiplier, offset_shift, k == 0)
            term = jnp.dot(weights, other_unit, preferred_element_type=jnp.float32)
            grad = term if grad is None else grad + term
        return project_back(grad, *normalize(own))

    d_images = side(picture_embeds, [text_before, text_diag], caption_embeds, True)
    d_texts = side(caption_embeds, [image_after, image_diag], picture_embeds, True)
    return (d_images, d_texts)


def solution(mesh):
    placed = (P(("row", "col"), None), P(("row", "col"), None), P(), P())
    return jax.shard_map(
        per_device,
        mesh=mesh,
        in_specs=placed,
        out_specs=(P(("row", "col"), None), P(("row", "col"), None)),
        check_vma=False,
    )
```

time: 173 us -> 114 us (0.66)
  waiting for transfers between devices: 119 us -> 58.5 us
  matrix products: 3.47 us -> 13.5 us
  starting transfers between devices: 40.5 us -> 32.4 us
    ppermute x4, waiting for transfers between devices: 119 us -> 58.5 us  [moved(): return lax.ppermute(block, AXES, route)]
    dot_general x9 -> x6, matrix products: 3.47 us -> 13.5 us  [side(): term = jnp.dot(weights, other_unit, preferred_element_type=jnp.float32)]
    ppermute x4, starting transfers between devices: 40.5 us -> 32.4 us  [moved(): return lax.ppermute(block, AXES, route)]
    reduce_sum x2 -> x6, other arithmetic: 1.52 us -> 3.3 us  [normalize(): norm = jnp.sqrt(jnp.sum(values * values, axis=-1, keepdims=True) + 1e-06)]
  transfers between devices with their start and end apart: 4 -> 4, of which waited for: 4 -> 3; matrix products, arithmetic and copies ran while one was open for 2% -> 7% of each run, Pallas kernels for 0% -> 0%
where the time goes in v1:
time: 114 us; the launch traced here: 113 us
  waiting for transfers between devices  58.5 us (51%)
  starting transfers between devices  32.4 us (28%)
  matrix products  13.5 us (12%)
  other arithmetic  7.09 us (6%)
  between operations  2.02 us (2%)
    ppermute x4, waiting for transfers between devices, moved(): return lax.ppermute(block, AXES, route)  58.5 us
    ppermute x4, starting transfers between devices, moved(): return lax.ppermute(block, AXES, route)  32.4 us
    dot_general x6, matrix products, side(): term = jnp.dot(weights, other_unit, preferred_element_type=jnp.float32)  13.5 us
    reduce_sum x6, other arithmetic, normalize(): norm = jnp.sqrt(jnp.sum(values * values, axis=-1, keepdims=True) + 1e-06)  3.3 us
    div x2, other arithmetic, project_back(): return (grad_unit - unit_float * inner) / norm  2.59 us
  transfers between devices with their start and end apart: 4, of which 3 were waited for; matrix products, arithmetic and copies ran while one was open for 7% of the time, Pallas kernels for 0%

profile of v1, /device:TPU:1, one launch (start us, length us, event | category | flops | bytes accessed | tf_op | source)
XLA Modules:
  0.0 113.5 jit_solution(7298991924014993623)
XLA Ops:
  0.6 0.0 copy-start
  0.7 12.6 %collective-permute-start.2 = (bf16[256,1152]{1,0:T(8,128)(2,1)}, bf16[256,1152]{1,0:T(8,128)(2,1)S(1)}, u32[]{:S(2)}, u32[]{:S(2)}) collective-permute-start(bf16[256,1152]{1,0:T(8,128)(2,1)} %param.4), channel_id=1, source_target_pairs={{0,752},{1,753},{2,754},{3,755},{4,756},{5,757},{6,758},{7,759},{8... | collective-permute-start | bytes 1769480 | tf_op jit(solution)/shard_map/ppermute | solution.py:17
  13.2 16.0 %collective-permute-start.3 = (bf16[256,1152]{1,0:T(8,128)(2,1)}, bf16[256,1152]{1,0:T(8,128)(2,1)S(1)}, u32[]{:S(2)}, u32[]{:S(2)}) collective-permute-start(bf16[256,1152]{1,0:T(8,128)(2,1)} %param.4), channel_id=1, source_target_pairs={{0,767},{1,752},{2,753},{3,754},{4,755},{5,756},{6,757},{7,758},{8... | collective-permute-start | bytes 1769480 | tf_op jit(solution)/shard_map/ppermute | solution.py:17
  29.2 1.9 %collective-permute-start = (bf16[256,1152]{1,0:T(8,128)(2,1)}, bf16[256,1152]{1,0:T(8,128)(2,1)S(1)}, u32[]{:S(2)}, u32[]{:S(2)}) collective-permute-start(bf16[256,1152]{1,0:T(8,128)(2,1)} %param.5), channel_id=1, source_target_pairs={{0,16},{1,17},{2,18},{3,19},{4,20},{5,21},{6,22},{7,23},{8,24},{9,... | collective-permute-start | bytes 1769480 | tf_op jit(solution)/shard_map/ppermute | solution.py:17
  31.1 1.9 %collective-permute-start.1 = (bf16[256,1152]{1,0:T(8,128)(2,1)}, bf16[256,1152]{1,0:T(8,128)(2,1)S(1)}, u32[]{:S(2)}, u32[]{:S(2)}) collective-permute-start(bf16[256,1152]{1,0:T(8,128)(2,1)} %param.5), channel_id=1, source_target_pairs={{0,17},{1,18},{2,19},{3,20},{4,21},{5,22},{6,23},{7,24},{8,25},{9,... | collective-permute-start | bytes 1769480 | tf_op jit(solution)/shard_map/ppermute | solution.py:17
  33.1 1.3 %fusion = f32[256]{0:T(256)S(1)} fusion(bf16[256,1152]{1,0:T(8,128)(2,1)} %param.4), kind=kLoop, calls=%fused_computation.16 | loop fusion | flops 884480 | bytes 590848 | tf_op jit(solution)/shard_map/reduce_sum | solution.py:22
  34.3 1.3 %fusion.1 = f32[256]{0:T(256)S(1)} fusion(bf16[256,1152]{1,0:T(8,128)(2,1)} %param.5), kind=kLoop, calls=%fused_computation.17 | loop fusion | flops 884480 | bytes 590848 | tf_op jit(solution)/shard_map/reduce_sum | solution.py:22
  36.9 2.0 %fusion.54 = f32[256,1152]{1,0:T(8,128)} fusion(f32[]{:T(128)S(6)} %div.47, f32[]{:T(128)} %bitcast.12, f32[]{:T(128)} %bitcast.6, f32[256]{0:T(256)S(1)} %get-tuple-element.6, bf16[256,1152]{1,0:T(8,128)(2,1)S(1)} %copy-done, f32[256]{0:T(256)S(1)} %get-tuple-element.7, bf16[256,1152]{1,0:T(8,128)(2,1)S(1)} %copy-done.1), kind=kOutput, calls=%fused_computation.80 | convolution fusion | flops 305299456 | bytes 2361356 | tf_op jit(solution)/shard_map/dot_general | solution.py:57
  39.0 2.0 %fusion.55 = f32[256,1152]{1,0:T(8,128)} fusion(f32[]{:T(128)S(6)} %div.47, f32[]{:T(128)} %bitcast.9, f32[]{:T(128)} %bitcast.2, f32[256]{0:T(256)S(1)} %get-tuple-element.6, bf16[256,1152]{1,0:T(8,128)(2,1)S(1)} %copy-done, f32[256]{0:T(256)S(1)} %get-tuple-element.7, bf16[256,1152]{1,0:T(8,128)(2,1)S(1)} %copy-done.1), kind=kOutput, calls=%fused_computation.81 | convolution fusion | flops 305299456 | bytes 2361356 | tf_op jit(solution)/shard_map/dot_general | solution.py:57
  41.0 0.2 fusion.6
  41.2 44.7 %collective-permute-done.3 = bf16[256,1152]{1,0:T(8,128)(2,1)S(1)} collective-permute-done((bf16[256,1152]{1,0:T(8,128)(2,1)}, bf16[256,1152]{1,0:T(8,128)(2,1)S(1)}, u32[]{:S(2)}, u32[]{:S(2)}) %collective-permute-start.3) | collective-permute-done | bytes 589856 | tf_op jit(solution)/shard_map/ppermute | solution.py:17
  85.9 0.2 fusion.8
  86.1 4.3 %collective-permute-done = bf16[256,1152]{1,0:T(8,128)(2,1)S(1)} collective-permute-done((bf16[256,1152]{1,0:T(8,128)(2,1)}, bf16[256,1152]{1,0:T(8,128)(2,1)S(1)}, u32[]{:S(2)}, u32[]{:S(2)}) %collective-permute-start) | collective-permute-done | bytes 589856 | tf_op jit(solution)/shard_map/ppermute | solution.py:17
  90.4 0.2 fusion.2
  90.6 0.6 add_sqrt_fusion
  91.1 0.6 add_sqrt_fusion.3
  91.7 9.5 %collective-permute-done.1 = bf16[256,1152]{1,0:T(8,128)(2,1)S(1)} collective-permute-done((bf16[256,1152]{1,0:T(8,128)(2,1)}, bf16[256,1152]{1,0:T(8,128)(2,1)S(1)}, u32[]{:S(2)}, u32[]{:S(2)}) %collective-permute-start.1) | collective-permute-done | bytes 589856 | tf_op jit(solution)/shard_map/ppermute | solution.py:17
  101.2 0.2 fusion.4
  101.4 3.3 %convolution_add_fusion.1 = f32[256,1152]{1,0:T(8,128)} fusion(f32[256,1152]{1,0:T(8,128)} %fusion.54, bf16[256,1152]{1,0:T(8,128)(2,1)S(1)} %collective-permute-done.2, f32[256]{0:T(256)S(1)} %add_sqrt_fusion.1, f32[]{:T(128)S(6)} %div.47, f32[]{:T(128)} %bitcast.11, f32[]{:T(128)} %bitcast.5, f32[256]{0:T(256)S(1)} %get-tuple-element.6, ...), kind=kOutput, calls=%fused_computation.1 | convolution fusion | flops 305397760 | bytes 3541004 | tf_op jit(solution)/shard_map/dot_general | solution.py:57
  104.8 2.7 %multiply_reduce_fusion = (f32[256]{0:T(256)S(1)}, f32[256,1152]{1,0:T(8,128)S(1)}) fusion(f32[256]{0:T(256)S(1)} %get-tuple-element.6, bf16[256,1152]{1,0:T(8,128)(2,1)S(1)} %copy-done, f32[256,1152]{1,0:T(8,128)} %convolution_add_fusion.1, bf16[256,1152]{1,0:T(8,128)(2,1)} %copy-done.2, f32[256]{0:T(256)} %add_sqrt_fusion, f32[]{:T(128)S(6)} %div.47, ...), kind=kOutput, calls=%fused_computation.27 | convolution fusion | flops 306577152 | bytes 3542028 | tf_op jit(solution)/shard_map/dot_general | solution.py:57
  107.5 1.3 %subtract_divide_fusion = f32[256,1152]{1,0:T(8,128)} fusion(f32[256,1152]{1,0:T(8,128)S(1)} %get-tuple-element.5, f32[256]{0:T(256)S(1)} %get-tuple-element.4, f32[256]{0:T(256)S(1)} %get-tuple-element.6, bf16[256,1152]{1,0:T(8,128)(2,1)S(1)} %copy-done), kind=kLoop, calls=%fused_computation.26 | loop fusion | flops 1474560 | bytes 2951168 | tf_op jit(solution)/shard_map/div | solution.py:42
  108.8 2.3 %convolution_add_fusion.3 = f32[256,1152]{1,0:T(8,128)S(1)} fusion(f32[256,1152]{1,0:T(8,128)} %fusion.55, bf16[256,1152]{1,0:T(8,128)(2,1)S(1)} %collective-permute-done, f32[256]{0:T(256)} %add_sqrt_fusion.3, f32[]{:T(128)S(6)} %div.47, f32[]{:T(128)} %bitcast.14, f32[]{:T(128)} %bitcast.8, f32[256]{0:T(256)S(1)} %get-tuple-element.7, ...), kind=kOutput, calls=%fused_computation.3 | convolution fusion | flops 305397760 | bytes 3541004 | tf_op jit(solution)/shard_map/dot_general | solution.py:57
  111.1 1.1 multiply_reduce_fusion.1
  112.2 1.3 %subtract_divide_fusion.1 = f32[256,1152]{1,0:T(8,128)} fusion(f32[256,1152]{1,0:T(8,128)S(1)} %get-tuple-element.3, f32[256]{0:T(256)S(1)} %get-tuple-element.2, f32[256]{0:T(256)S(1)} %get-tuple-element.7, bf16[256,1152]{1,0:T(8,128)(2,1)S(1)} %copy-done.1), kind=kLoop, calls=%fused_computation.28 | loop fusion | flops 1474560 | bytes 2951168 | tf_op jit(solution)/shard_map/div | solution.py:42
  (9 shorter events, 0.0 us)
Async XLA Ops:
  0.6 36.3 %copy-start.1 = (bf16[256,1152]{1,0:T(8,128)(2,1)S(1)}, bf16[256,1152]{1,0:T(8,128)(2,1)}, u32[]{:S(2)}) copy-start(bf16[256,1152]{1,0:T(8,128)(2,1)} %param.4) | copy-start | bytes 1769476
  0.6 36.3 %copy-start = (bf16[256,1152]{1,0:T(8,128)(2,1)S(1)}, bf16[256,1152]{1,0:T(8,128)(2,1)}, u32[]{:S(2)}) copy-start(bf16[256,1152]{1,0:T(8,128)(2,1)} %param.5) | copy-start | bytes 1769476
  0.7 40.3 %collective-permute-start.2 = (bf16[256,1152]{1,0:T(8,128)(2,1)}, bf16[256,1152]{1,0:T(8,128)(2,1)S(1)}, u32[]{:S(2)}, u32[]{:S(2)}) collective-permute-start(bf16[256,1152]{1,0:T(8,128)(2,1)} %param.4), channel_id=1, source_target_pairs={{0,752},{1,753},{2,754},{3,755},{4,756},{5,757},{6,758},{7,759},{8... | collective-permute-start | bytes 1769480 | tf_op jit(solution)/shard_map/ppermute | solution.py:17
  13.2 72.6 %collective-permute-start.3 = (bf16[256,1152]{1,0:T(8,128)(2,1)}, bf16[256,1152]{1,0:T(8,128)(2,1)S(1)}, u32[]{:S(2)}, u32[]{:S(2)}) collective-permute-start(bf16[256,1152]{1,0:T(8,128)(2,1)} %param.4), channel_id=1, source_target_pairs={{0,767},{1,752},{2,753},{3,754},{4,755},{5,756},{6,757},{7,758},{8... | collective-permute-start | bytes 1769480 | tf_op jit(solution)/shard_map/ppermute | solution.py:17
  29.2 61.1 %collective-permute-start = (bf16[256,1152]{1,0:T(8,128)(2,1)}, bf16[256,1152]{1,0:T(8,128)(2,1)S(1)}, u32[]{:S(2)}, u32[]{:S(2)}) collective-permute-start(bf16[256,1152]{1,0:T(8,128)(2,1)} %param.5), channel_id=1, source_target_pairs={{0,16},{1,17},{2,18},{3,19},{4,20},{5,21},{6,22},{7,23},{8,24},{9,... | collective-permute-start | bytes 1769480 | tf_op jit(solution)/shard_map/ppermute | solution.py:17
  31.1 70.1 %collective-permute-start.1 = (bf16[256,1152]{1,0:T(8,128)(2,1)}, bf16[256,1152]{1,0:T(8,128)(2,1)S(1)}, u32[]{:S(2)}, u32[]{:S(2)}) collective-permute-start(bf16[256,1152]{1,0:T(8,128)(2,1)} %param.5), channel_id=1, source_target_pairs={{0,17},{1,18},{2,19},{3,20},{4,21},{5,22},{6,23},{7,24},{8,25},{9,... | collective-permute-start | bytes 1769480 | tf_op jit(solution)/shard_map/ppermute | solution.py:17
  85.9 18.9 %copy-start.2 = (bf16[256,1152]{1,0:T(8,128)(2,1)}, bf16[256,1152]{1,0:T(8,128)(2,1)S(1)}, u32[]{:S(2)}) copy-start(bf16[256,1152]{1,0:T(8,128)(2,1)S(1)} %collective-permute-done.3) | copy-start | bytes 1769476

commit v2 on v1

v2 whole, which is shorter than its diff:
```python
import functools

import jax
import jax.numpy as jnp
from jax import lax
from jax.experimental import pallas as pl
from jax.experimental.pallas import tpu as pltpu
from jax.sharding import PartitionSpec as P

AXES = ("row", "col")


def moved(block, rows_on, cols_on):
    n_row, n_col = (lax.axis_size(a) for a in AXES)
    route = [
        (r * n_col + c, (r + rows_on) % n_row * n_col + (c + cols_on) % n_col)
        for r in range(n_row)
        for c in range(n_col)
    ]
    return lax.ppermute(block, AXES, route)


def inverse_norm(values):
    return 1.0 / jnp.sqrt(jnp.sum(values * values, axis=-1, keepdims=True) + 1e-06)


def unit(block):
    values = block.astype(jnp.float32)
    return (values * inverse_norm(values)).astype(jnp.bfloat16)


def weights_of(left, right, multiplier, shift, matched):
    cosine = lax.dot_general(
        left, right, (((1,), (1,)), ((), ())), preferred_element_type=jnp.float32
    )
    share = 1.0 / (1.0 + jnp.exp(-(multiplier * cosine + shift)))
    if matched:
        at = [lax.broadcasted_iota(jnp.int32, share.shape, d) for d in (0, 1)]
        share = jnp.where(at[0] == at[1], share - 1.0, share)
    return (share * (multiplier / left.shape[0])).astype(jnp.bfloat16)


def own_kernel(multiplier, shift, image, text, d_image, d_text):
    image_unit, text_unit = unit(image[...]), unit(text[...])
    for own, other, out in ((image_unit, text_unit, d_image), (text_unit, image_unit, d_text)):
        weights = weights_of(own, other, multiplier[0], shift[0], True)
        out[...] = jnp.dot(weights, other, preferred_element_type=jnp.float32)


def side_kernel(multiplier, shift, far, near, own, start, out, total, sems):
    rows = own.shape[0]
    values = own[...].astype(jnp.float32)
    inverse = inverse_norm(values)
    own_unit = (values * inverse).astype(jnp.bfloat16)
    grad = start[...]
    for block in (near, far):
        other = unit(block[...])
        weights = weights_of(own_unit, other, multiplier[0], shift[0], False)
        grad = grad + jnp.dot(weights, other, preferred_element_type=jnp.float32)
    total[...] = grad
    parts = sems.shape[0]
    copies = []
    for i in range(parts):
        part = slice(i * rows // parts, (i + 1) * rows // parts)
        own_float = own[part].astype(jnp.float32) * inverse[part]
        grad = total[part]
        inner = jnp.sum(own_float * grad, axis=-1, keepdims=True)
        total[part] = (grad - own_float * inner) * inverse[part]
        copy = pltpu.make_async_copy(total.at[part], out.at[part], sems.at[i])
        copy.start()
        copies.append(copy)
    for copy in copies:
        copy.wait()


SCALAR = pl.BlockSpec(memory_space=pltpu.SMEM)
WHOLE = pl.BlockSpec(memory_space=pltpu.VMEM)
PARAMS = pltpu.CompilerParams(vmem_limit_bytes=32 << 20)
PARTS = 4


def own_call(*operands):
    grad = jax.ShapeDtypeStruct(operands[-1].shape, jnp.float32)
    return pl.pallas_call(
        own_kernel,
        out_shape=(grad, grad),
        in_specs=[SCALAR] * 2 + [WHOLE] * 2,
        out_specs=[WHOLE] * 2,
        compiler_params=PARAMS,
        name="own",
    )(*operands)


def side_call(*operands):
    grad = jax.ShapeDtypeStruct(operands[-1].shape, jnp.float32)
    return pl.pallas_call(
        side_kernel,
        out_shape=grad,
        in_specs=[SCALAR] * 2 + [WHOLE] * 4,
        out_specs=pl.BlockSpec(memory_space=pl.ANY),
        scratch_shapes=[
            pltpu.VMEM(grad.shape, jnp.float32),
            pltpu.SemaphoreType.DMA((PARTS,)),
        ],
        compiler_params=PARAMS,
        name="side",
    )(*operands)


def per_device(picture_embeds, caption_embeds, logit_multiplier, offset_shift):
    scalars = (logit_multiplier, offset_shift)
    text_far = moved(caption_embeds, 1, 1)
    image_far = moved(picture_embeds, -1, -1)
    text_near = moved(caption_embeds, 1, 0)
    image_near = moved(picture_embeds, -1, 0)
    image_start, text_start = own_call(*scalars, picture_embeds, caption_embeds)
    d_images = side_call(*scalars, text_far, text_near, picture_embeds, image_start)
    d_texts = side_call(*scalars, image_far, image_near, caption_embeds, text_start)
    return (d_images, d_texts)


def solution(mesh):
    placed = (P(("row", "col"), None), P(("row", "col"), None), P(), P())
    return jax.shard_map(
        per_device,
        mesh=mesh,
        in_specs=placed,
        out_specs=(P(("row", "col"), None), P(("row", "col"), None)),
        check_vma=False,
    )
```

time: 114 us -> 103 us (0.904)
  matrix products: 13.5 us -> 0 us
  Pallas kernels: 0 us -> 7.74 us
  other arithmetic: 7.09 us -> 0 us
  waiting for transfers between devices: 58.5 us -> 64.5 us
  starting transfers between devices: 32.4 us -> 26.6 us
  local copies, waits for them, and re-layouts: 0.01 us -> 2.12 us
    dot_general x6 -> x0, matrix products: 13.5 us -> none  [side(): term = jnp.dot(weights, other_unit, preferred_element_type=jnp.float32)]
    pallas_call x0 -> x3, Pallas kernels: none -> 7.74 us  [the longest x2 5.78 us: side_call(): pl.pallas_call(side_kernel, out_shape=grad, in_specs=[SCALAR] * 2 + [WHOL...]
    ppermute x4, waiting for transfers between devices: 58.5 us -> 64.5 us  [moved(): return lax.ppermute(block, AXES, route)]
    ppermute x4, starting transfers between devices: 32.4 us -> 26.6 us  [moved(): return lax.ppermute(block, AXES, route)]
    reduce_sum x6 -> x0, other arithmetic: 3.3 us -> none  [normalize(): norm = jnp.sqrt(jnp.sum(values * values, axis=-1, keepdims=True) + 1e-06)]
    div x2 -> x0, other arithmetic: 2.59 us -> none  [project_back(): return (grad_unit - unit_float * inner) / norm]
    unnamed x6, local copies, waits for them, and re-layouts: 0.01 us -> 2.12 us
    sqrt x5 -> x0, other arithmetic: 1.2 us -> none  [normalize(): norm = jnp.sqrt(jnp.sum(values * values, axis=-1, keepdims=True) + 1e-06)]
  transfers between devices with their start and end apart: 4 -> 4, of which waited for: 3 -> 2; matrix products, arithmetic and copies ran while one was open for 7% -> 0% of each run, Pallas kernels for 0% -> 5%
where the time goes in v2:
time: 103 us
  waiting for transfers between devices  64.5 us (63%)
  starting transfers between devices  26.6 us (26%)
  Pallas kernels  7.74 us (8%)
  local copies, waits for them, and re-layouts  2.12 us (2%)
  between operations  1.98 us (2%)
    ppermute x4, waiting for transfers between devices, moved(): return lax.ppermute(block, AXES, route)  64.5 us
    ppermute x4, starting transfers between devices, moved(): return lax.ppermute(block, AXES, route)  26.6 us
    pallas_call x2, Pallas kernels, side_call(): pl.pallas_call(side_kernel, out_shape=grad, in_specs=[SCALAR] * 2 + [WHOL...  5.78 us
    unnamed x6, local copies, waits for them, and re-layouts  2.12 us
  transfers between devices with their start and end apart: 4, of which 2 were waited for; matrix products, arithmetic and copies ran while one was open for 0% of the time, Pallas kernels for 5%

profile of v2, /device:TPU:1, one launch (start us, length us, event | category | flops | bytes accessed | tf_op | source)
XLA Modules:
  0.0 103.0 jit_solution(17283578913307544381)
XLA Ops:
  0.6 19.2 %collective-permute-start.2 = (bf16[256,1152]{1,0:T(8,128)(2,1)}, bf16[256,1152]{1,0:T(8,128)(2,1)S(1)}, u32[]{:S(2)}, u32[]{:S(2)}) collective-permute-start(bf16[256,1152]{1,0:T(8,128)(2,1)} %own.4), channel_id=1, source_target_pairs={{0,767},{1,752},{2,753},{3,754},{4,755},{5,756},{6,757},{7,758},{8... | collective-permute-start | bytes 1769480 | tf_op jit(solution)/shard_map/ppermute | solution.py:20
  19.8 3.4 %collective-permute-start.3 = (bf16[256,1152]{1,0:T(8,128)(2,1)}, bf16[256,1152]{1,0:T(8,128)(2,1)S(1)}, u32[]{:S(2)}, u32[]{:S(2)}) collective-permute-start(bf16[256,1152]{1,0:T(8,128)(2,1)} %own.4), channel_id=1, source_target_pairs={{0,752},{1,753},{2,754},{3,755},{4,756},{5,757},{6,758},{7,759},{8... | collective-permute-start | bytes 1769480 | tf_op jit(solution)/shard_map/ppermute | solution.py:20
  23.2 1.9 %collective-permute-start = (bf16[256,1152]{1,0:T(8,128)(2,1)}, bf16[256,1152]{1,0:T(8,128)(2,1)S(1)}, u32[]{:S(2)}, u32[]{:S(2)}) collective-permute-start(bf16[256,1152]{1,0:T(8,128)(2,1)} %own.5), channel_id=1, source_target_pairs={{0,17},{1,18},{2,19},{3,20},{4,21},{5,22},{6,23},{7,24},{8,25},{9,... | collective-permute-start | bytes 1769480 | tf_op jit(solution)/shard_map/ppermute | solution.py:20
  25.1 2.2 %collective-permute-start.1 = (bf16[256,1152]{1,0:T(8,128)(2,1)}, bf16[256,1152]{1,0:T(8,128)(2,1)S(1)}, u32[]{:S(2)}, u32[]{:S(2)}) collective-permute-start(bf16[256,1152]{1,0:T(8,128)(2,1)} %own.5), channel_id=1, source_target_pairs={{0,16},{1,17},{2,18},{3,19},{4,20},{5,21},{6,22},{7,23},{8,24},{9,... | collective-permute-start | bytes 1769480 | tf_op jit(solution)/shard_map/ppermute | solution.py:20
  28.6 0.0 copy-start
  28.6 1.1 %copy-done = bf16[256,1152]{1,0:T(8,128)(2,1)S(1)} copy-done((bf16[256,1152]{1,0:T(8,128)(2,1)S(1)}, bf16[256,1152]{1,0:T(8,128)(2,1)}, u32[]{:S(2)}) %copy-start) | copy-done | bytes 589848
  29.7 0.0 copy-start.2
  29.7 1.1 %copy-done.2 = bf16[256,1152]{1,0:T(8,128)(2,1)S(1)} copy-done((bf16[256,1152]{1,0:T(8,128)(2,1)S(1)}, bf16[256,1152]{1,0:T(8,128)(2,1)}, u32[]{:S(2)}) %copy-start.2) | copy-done | bytes 589848
  30.7 0.0 copy-start.1
  30.7 2.0 %own.3 = (f32[256,1152]{1,0:T(8,128)S(1)}, f32[256,1152]{1,0:T(8,128)S(1)}) custom-call(f32[1]{0:T(128)S(6)} %copy.6.multiplier, f32[1]{0:T(128)S(6)} %copy.7.shift, bf16[256,1152]{1,0:T(8,128)(2,1)S(1)} %copy-done.2, bf16[256,1152]{1,0:T(8,128)(2,1)S(1)} %copy-done), custom_call_target="tpu_custom_call" | custom-call | tf_op jit(solution)/shard_map/own/pallas_call | solution.py:84
  32.7 27.7 %collective-permute-done.2.far = bf16[256,1152]{1,0:T(8,128)(2,1)S(1)} collective-permute-done((bf16[256,1152]{1,0:T(8,128)(2,1)}, bf16[256,1152]{1,0:T(8,128)(2,1)S(1)}, u32[]{:S(2)}, u32[]{:S(2)}) %collective-permute-start.2) | collective-permute-done | bytes 589856 | tf_op jit(solution)/shard_map/ppermute | solution.py:20
  60.4 0.0 collective-permute-done.3.near
  60.4 0.0 copy-done.1
  60.4 2.9 %side.3 = f32[256,1152]{1,0:T(8,128)} custom-call(f32[1]{0:T(128)S(6)} %copy.6.multiplier, f32[1]{0:T(128)S(6)} %copy.7.shift, bf16[256,1152]{1,0:T(8,128)(2,1)S(1)} %collective-permute-done.2.far, bf16[256,1152]{1,0:T(8,128)(2,1)S(1)} %collective-permute-done.3.near, bf16[256,1152]{1,0:T(8,128)(2,1)S(1)} %copy-done.1, f32[256,1152]{1,0:T(8,128)S(1)} %get-tuple-element.5.start), custom_call_target="tpu_custom_call" | custom-call | tf_op jit(solution)/shard_map/side/pallas_call | solution.py:96
  63.3 36.8 %collective-permute-done.far = bf16[256,1152]{1,0:T(8,128)(2,1)S(1)} collective-permute-done((bf16[256,1152]{1,0:T(8,128)(2,1)}, bf16[256,1152]{1,0:T(8,128)(2,1)S(1)}, u32[]{:S(2)}, u32[]{:S(2)}) %collective-permute-start) | collective-permute-done | bytes 589856 | tf_op jit(solution)/shard_map/ppermute | solution.py:20
  100.1 0.0 collective-permute-done.1.near
  100.1 2.9 %side.2 = f32[256,1152]{1,0:T(8,128)} custom-call(f32[1]{0:T(128)S(6)} %copy.6.multiplier, f32[1]{0:T(128)S(6)} %copy.7.shift, bf16[256,1152]{1,0:T(8,128)(2,1)S(1)} %collective-permute-done.far, bf16[256,1152]{1,0:T(8,128)(2,1)S(1)} %collective-permute-done.1.near, bf16[256,1152]{1,0:T(8,128)(2,1)S(1)} %copy-done.2, f32[256,1152]{1,0:T(8,128)S(1)} %get-tuple-element.4.start), custom_call_target="tpu_custom_call" | custom-call | tf_op jit(solution)/shard_map/side/pallas_call | solution.py:96
Async XLA Ops:
  0.6 59.8 %collective-permute-start.2 = (bf16[256,1152]{1,0:T(8,128)(2,1)}, bf16[256,1152]{1,0:T(8,128)(2,1)S(1)}, u32[]{:S(2)}, u32[]{:S(2)}) collective-permute-start(bf16[256,1152]{1,0:T(8,128)(2,1)} %own.4), channel_id=1, source_target_pairs={{0,767},{1,752},{2,753},{3,754},{4,755},{5,756},{6,757},{7,758},{8... | collective-permute-start | bytes 1769480 | tf_op jit(solution)/shard_map/ppermute | solution.py:20
  19.8 40.6 %collective-permute-start.3 = (bf16[256,1152]{1,0:T(8,128)(2,1)}, bf16[256,1152]{1,0:T(8,128)(2,1)S(1)}, u32[]{:S(2)}, u32[]{:S(2)}) collective-permute-start(bf16[256,1152]{1,0:T(8,128)(2,1)} %own.4), channel_id=1, source_target_pairs={{0,752},{1,753},{2,754},{3,755},{4,756},{5,757},{6,758},{7,759},{8... | collective-permute-start | bytes 1769480 | tf_op jit(solution)/shard_map/ppermute | solution.py:20
  23.2 76.9 %collective-permute-start = (bf16[256,1152]{1,0:T(8,128)(2,1)}, bf16[256,1152]{1,0:T(8,128)(2,1)S(1)}, u32[]{:S(2)}, u32[]{:S(2)}) collective-permute-start(bf16[256,1152]{1,0:T(8,128)(2,1)} %own.5), channel_id=1, source_target_pairs={{0,17},{1,18},{2,19},{3,20},{4,21},{5,22},{6,23},{7,24},{8,25},{9,... | collective-permute-start | bytes 1769480 | tf_op jit(solution)/shard_map/ppermute | solution.py:20
  25.1 75.0 %collective-permute-start.1 = (bf16[256,1152]{1,0:T(8,128)(2,1)}, bf16[256,1152]{1,0:T(8,128)(2,1)S(1)}, u32[]{:S(2)}, u32[]{:S(2)}) collective-permute-start(bf16[256,1152]{1,0:T(8,128)(2,1)} %own.5), channel_id=1, source_target_pairs={{0,16},{1,17},{2,18},{3,19},{4,20},{5,21},{6,22},{7,23},{8,24},{9,... | collective-permute-start | bytes 1769480 | tf_op jit(solution)/shard_map/ppermute | solution.py:20
  28.6 1.1 %copy-start = (bf16[256,1152]{1,0:T(8,128)(2,1)S(1)}, bf16[256,1152]{1,0:T(8,128)(2,1)}, u32[]{:S(2)}) copy-start(bf16[256,1152]{1,0:T(8,128)(2,1)} %own.5) | copy-start | bytes 1769476
  29.7 1.1 %copy-start.2 = (bf16[256,1152]{1,0:T(8,128)(2,1)S(1)}, bf16[256,1152]{1,0:T(8,128)(2,1)}, u32[]{:S(2)}) copy-start(bf16[256,1152]{1,0:T(8,128)(2,1)} %own.4) | copy-start | bytes 1769476
  30.7 29.7 %copy-start.1 = (bf16[256,1152]{1,0:T(8,128)(2,1)S(1)}, bf16[256,1152]{1,0:T(8,128)(2,1)}, u32[]{:S(2)}) copy-start(bf16[256,1152]{1,0:T(8,128)(2,1)} %own.5) | copy-start | bytes 1769476

commit v3 on v1

v3 whole, which is shorter than its diff:
```python
import jax
import jax.numpy as jnp
from jax import lax
from jax.experimental import pallas as pl
from jax.experimental.pallas import tpu as pltpu
from jax.sharding import PartitionSpec as P

AXES = ("row", "col")
FIRST = 0
WIDTH = 256


def swapped(block, cols_on, parity, columns=None):
    n_row, n_col = (lax.axis_size(a) for a in AXES)
    route = []
    for r in range(parity, n_row, 2):
        for c in range(n_col):
            if columns is not None and c % 2 != columns:
                continue
            here = r * n_col + c
            there = (r + 1) % n_row * n_col + (c + cols_on) % n_col
            route += [(here, there), (there, here)]
    return lax.ppermute(block, AXES, route)


def inverse_norm(values):
    return 1.0 / jnp.sqrt(jnp.sum(values * values, axis=-1, keepdims=True) + 1e-06)


def unit(block):
    values = block.astype(jnp.float32)
    return (values * inverse_norm(values)).astype(jnp.bfloat16)


def cosines(left, right):
    return lax.dot_general(
        left, right, (((1,), (1,)), ((), ())), preferred_element_type=jnp.float32
    )


def weights_of(cosine, multiplier, shift, matched=False):
    share = 1.0 / (1.0 + jnp.exp(-(multiplier[0] * cosine + shift[0])))
    if matched:
        at = [lax.broadcasted_iota(jnp.int32, share.shape, d) for d in (0, 1)]
        share = jnp.where(at[0] == at[1], share - 1.0, share)
    return (share * (multiplier[0] / cosine.shape[0])).astype(jnp.bfloat16)


def tile_sum(own_unit, other_unit, multiplier, shift, matched=False):
    weights = weights_of(cosines(own_unit, other_unit), multiplier, shift, matched)
    return jnp.dot(weights, other_unit, preferred_element_type=jnp.float32)


def own_kernel(multiplier, shift, first, second, near, *outs):
    d_first, d_second, own_unit, rest, inverse_out, inner_out = outs
    first_unit = unit(first[...])
    values = second[...].astype(jnp.float32)
    inverse = inverse_norm(values)
    own_float = values * inverse
    second_unit = own_float.astype(jnp.bfloat16)
    d_first[...] = tile_sum(first_unit, second_unit, multiplier, shift, True)
    grad = tile_sum(second_unit, first_unit, multiplier, shift, True) + tile_sum(
        second_unit, unit(near[...]), multiplier, shift
    )
    d_second[...] = grad
    own_unit[...] = second_unit
    rest[...] = (own_float - second_unit.astype(jnp.float32)).astype(jnp.bfloat16)
    inverse_out[...] = jnp.broadcast_to(inverse, inverse_out.shape)
    inner = jnp.sum(own_float * grad, axis=-1, keepdims=True)
    inner_out[...] = jnp.broadcast_to(inner, inner_out.shape)


def parts_of(width):
    return [slice(a, min(a + WIDTH, width)) for a in range(0, width, WIDTH)]


def write_out(action, parts, total, outs, chosen, sems):
    for i, out in enumerate(outs):

        @pl.when(chosen == i)
        def _():
            for k, part in parts:
                copy = pltpu.make_async_copy(total.at[:, part], out.at[:, part], sems.at[k])
                getattr(copy, action)()


def first_kernel(multiplier, shift, odd, own, start, far, near, d_images, d_texts, total, sems):
    values = own[...].astype(jnp.float32)
    inverse = inverse_norm(values)
    own_float = values * inverse
    own_unit = own_float.astype(jnp.bfloat16)
    grad = start[...]
    for block in (far, near):
        grad += tile_sum(own_unit, unit(block[...]), multiplier, shift)
    inner = jnp.sum(own_float * grad, axis=-1, keepdims=True)
    total[...] = (grad - own_float * inner) * inverse
    parts = list(enumerate(parts_of(own.shape[1])))
    image_side = jnp.where(odd[0] == FIRST, 0, 1)
    for action in ("start", "wait"):
        write_out(action, parts, total, (d_texts, d_images), image_side, sems)


def second_kernel(
    multiplier, shift, odd, late, own, start, own_unit, rest, inverse, inner, far, near, *refs
):
    d_images, d_texts, far_unit, near_sum, total, sems = refs[-6:]
    far_unit[...] = unit(far[...])
    cosine = cosines(own_unit[...], far_unit[...])
    weights = weights_of(cosine, multiplier, shift)
    exact = cosine + cosines(rest[...], far_unit[...])
    scale = inverse[:, :1]
    far_inner = inner[:, :1] + jnp.sum(
        weights.astype(jnp.float32) * exact, axis=-1, keepdims=True
    )
    parts = list(enumerate(parts_of(own.shape[1])))
    text_side = jnp.where(odd[0] == FIRST, 0, 1)

    def finish(begun, inner):
        inner = inner * scale
        for k, part in parts:
            grad = begun[:, part] + jnp.dot(
                weights, far_unit[:, part], preferred_element_type=jnp.float32
            )
            own_float = own[:, part].astype(jnp.float32) * scale
            total[:, part] = grad * scale - own_float * inner
            write_out("start", [(k, part)], total, (d_images, d_texts), text_side, sems)
        write_out("wait", parts, total, (d_images, d_texts), text_side, sems)

    @pl.when(late[0] == 0)
    def _():
        finish(start, far_inner)

    @pl.when(late[0] == 1)
    def _():
        grad = tile_sum(own_unit[...], unit(near[...]), multiplier, shift)
        near_sum[...] = start[...] + grad
        own_float = own[...].astype(jnp.float32) * scale
        finish(near_sum, far_inner + jnp.sum(own_float * grad, axis=-1, keepdims=True))


SCALAR = pl.BlockSpec(memory_space=pltpu.SMEM)
WHOLE = pl.BlockSpec(memory_space=pltpu.VMEM)
ANYWHERE = pl.BlockSpec(memory_space=pl.ANY)
PARAMS = pltpu.CompilerParams(vmem_limit_bytes=32 << 20)


def own_call(multiplier, shift, first, second, near):
    grad = jax.ShapeDtypeStruct(first.shape, jnp.float32)
    block = jax.ShapeDtypeStruct(first.shape, jnp.bfloat16)
    column = jax.ShapeDtypeStruct((first.shape[0], 128), jnp.float32)
    return pl.pallas_call(
        own_kernel,
        out_shape=(grad, grad, block, block, column, column),
        in_specs=[SCALAR] * 2 + [WHOLE] * 3,
        out_specs=[WHOLE] * 6,
        compiler_params=PARAMS,
        name="own",
    )(multiplier, shift, first, second, near)


def side_call(kernel, scalars, blocks, held, scratch, name):
    shape = blocks[0].shape
    grad = jax.ShapeDtypeStruct(shape, jnp.float32)
    operands = (*scalars, *blocks)
    return pl.pallas_call(
        kernel,
        out_shape=(grad, grad),
        in_specs=[SCALAR] * len(scalars) + [WHOLE] * len(blocks) + [ANYWHERE] * len(held),
        out_specs=[ANYWHERE] * 2,
        input_output_aliases={len(operands) + i: i for i in range(len(held))},
        scratch_shapes=[
            *(pltpu.VMEM(shape, dtype) for dtype in scratch),
            pltpu.VMEM(shape, jnp.float32),
            pltpu.SemaphoreType.DMA((len(parts_of(shape[1])),)),
        ],
        compiler_params=PARAMS,
        name=name,
    )(*operands, *held)


def per_device(picture_embeds, caption_embeds, logit_multiplier, offset_shift):
    scalars = (logit_multiplier, offset_shift)
    odd, late = ((lax.axis_index(a) % 2).astype(jnp.int32)[None] for a in AXES)
    first = jnp.where(odd == FIRST, caption_embeds, picture_embeds)
    second = jnp.where(odd == FIRST, picture_embeds, caption_embeds)
    early_near = swapped(second, 0, 1 - FIRST, 0)
    first_far, first_near = swapped(first, 1, FIRST), swapped(first, 0, FIRST)
    second_far = swapped(second, 1, 1 - FIRST)
    late_near = swapped(second, 0, 1 - FIRST, 1)
    first_start, *second_own = own_call(*scalars, first, second, early_near)
    held = side_call(
        first_kernel,
        (*scalars, odd),
        (first, first_start, first_far, first_near),
        (),
        (),
        "first",
    )
    return side_call(
        second_kernel,
        (*scalars, odd, late),
        (second, *second_own, second_far, late_near),
        held,
        (jnp.bfloat16, jnp.float32),
        "second",
    )


def solution(mesh):
    placed = (P(("row", "col"), None), P(("row", "col"), None), P(), P())
    return jax.shard_map(
        per_device,
        mesh=mesh,
        in_specs=placed,
        out_specs=(P(("row", "col"), None), P(("row", "col"), None)),
        check_vma=False,
    )
```

time: 114 us -> 99 us (0.87)
  matrix products: 13.5 us -> 0 us
  Pallas kernels: 0 us -> 8.23 us
  starting transfers between devices: 32.4 us -> 24.4 us
  other arithmetic: 7.09 us -> 1.35 us
  waiting for transfers between devices: 58.5 us -> 61.5 us
    dot_general x6 -> x0, matrix products: 13.5 us -> none  [side(): term = jnp.dot(weights, other_unit, preferred_element_type=jnp.float32)]
    pallas_call x0 -> x3, Pallas kernels: none -> 8.23 us  [the longest x2 6.12 us: side_call(): pl.pallas_call(kernel, out_shape=(grad, grad), in_specs=[SCALAR] * len(sc...]
    ppermute x4 -> x5, starting transfers between devices: 32.4 us -> 24.4 us  [swapped(): return lax.ppermute(block, AXES, route)]
    reduce_sum x6 -> x0, other arithmetic: 3.3 us -> none  [normalize(): norm = jnp.sqrt(jnp.sum(values * values, axis=-1, keepdims=True) + 1e-06)]
    ppermute x4 -> x5, waiting for transfers between devices: 58.5 us -> 61.5 us  [swapped(): return lax.ppermute(block, AXES, route)]
    div x2 -> x0, other arithmetic: 2.59 us -> none  [project_back(): return (grad_unit - unit_float * inner) / norm]
    select_n x0 -> x1, other arithmetic: none -> 1.35 us  [per_device(): first = jnp.where(odd == FIRST, caption_embeds, picture_embeds)]
    sqrt x5 -> x0, other arithmetic: 1.2 us -> none  [normalize(): norm = jnp.sqrt(jnp.sum(values * values, axis=-1, keepdims=True) + 1e-06)]
  transfers between devices with their start and end apart: 4 -> 5, of which waited for: 3 -> 2; matrix products, arithmetic and copies ran while one was open for 7% -> 0% of each run, Pallas kernels for 0% -> 6%
where the time goes in v3:
time: 99 us; the launch traced here: 97.5 us
  waiting for transfers between devices  61.5 us (62%)
  starting transfers between devices  24.4 us (25%)
  Pallas kernels  8.23 us (8%)
  between operations  2.01 us (2%)
  other arithmetic  1.35 us (1%)
    ppermute x5, waiting for transfers between devices, swapped(): return lax.ppermute(block, AXES, route)  61.5 us
    ppermute x5, starting transfers between devices, swapped(): return lax.ppermute(block, AXES, route)  24.4 us
    pallas_call x2, Pallas kernels, side_call(): pl.pallas_call(kernel, out_shape=(grad, grad), in_specs=[SCALAR] * len(sc...  6.12 us
    pallas_call x1, Pallas kernels, own_call(): pl.pallas_call(own_kernel, out_shape=(grad, grad, block, block, column, c...  2.11 us
  transfers between devices with their start and end apart: 5, of which 2 were waited for; matrix products, arithmetic and copies ran while one was open for 0% of the time, Pallas kernels for 6%

profile of v3, /device:TPU:1, one launch (start us, length us, event | category | flops | bytes accessed | tf_op | source)
XLA Modules:
  0.0 97.5 jit_solution(13172596378435527345)
XLA Ops:
  0.6 1.4 %broadcast_select_fusion = (bf16[256,1152]{1,0:T(8,128)(2,1)S(1)}, bf16[256,1152]{1,0:T(8,128)(2,1)S(1)}) fusion(bf16[256,1152]{1,0:T(8,128)(2,1)} %param.5, bf16[256,1152]{1,0:T(8,128)(2,1)} %param.4, pred[]{:T(512)} %bitcast.2), kind=kLoop, calls=%fused_computation | loop fusion | flops 589824 | bytes 2359297 | tf_op jit(solution)/shard_map/jit(_where)/select_n | solution.py:184
  2.0 5.4 %collective-permute-start = (bf16[256,1152]{1,0:T(8,128)(2,1)S(1)}, bf16[256,1152]{1,0:T(8,128)(2,1)S(1)}, u32[]{:S(2)}, u32[]{:S(2)}) collective-permute-start(bf16[256,1152]{1,0:T(8,128)(2,1)S(1)} %get-tuple-element.19.second.own), channel_id=1, source_target_pairs={{16,32},{32,16},{18,34},{34,18},{20,36},{36,20},{22,38},{38,22},{2... | collective-permute-start | bytes 1769480 | tf_op jit(solution)/shard_map/ppermute | solution.py:23
  7.4 14.5 %collective-permute-start.3 = (bf16[256,1152]{1,0:T(8,128)(2,1)S(1)}, bf16[256,1152]{1,0:T(8,128)(2,1)S(1)}, u32[]{:S(2)}, u32[]{:S(2)}) collective-permute-start(bf16[256,1152]{1,0:T(8,128)(2,1)S(1)} %get-tuple-element.18.first.own), channel_id=1, source_target_pairs={{0,17},{17,0},{1,18},{18,1},{2,19},{19,2},{3,20},{20,3},{4,21},{21... | collective-permute-start | bytes 1769480 | tf_op jit(solution)/shard_map/ppermute | solution.py:23
  21.9 1.9 %collective-permute-start.4 = (bf16[256,1152]{1,0:T(8,128)(2,1)S(1)}, bf16[256,1152]{1,0:T(8,128)(2,1)}, u32[]{:S(2)}, u32[]{:S(2)}) collective-permute-start(bf16[256,1152]{1,0:T(8,128)(2,1)S(1)} %get-tuple-element.18.first.own), channel_id=1, source_target_pairs={{0,16},{16,0},{1,17},{17,1},{2,18},{18,2},{3,19},{19,3},{4,20},{20... | collective-permute-start | bytes 1769480 | tf_op jit(solution)/shard_map/ppermute | solution.py:23
  23.8 1.9 %collective-permute-start.1 = (bf16[256,1152]{1,0:T(8,128)(2,1)S(1)}, bf16[256,1152]{1,0:T(8,128)(2,1)S(1)}, u32[]{:S(2)}, u32[]{:S(2)}) collective-permute-start(bf16[256,1152]{1,0:T(8,128)(2,1)S(1)} %get-tuple-element.19.second.own), channel_id=1, source_target_pairs={{16,33},{33,16},{17,34},{34,17},{18,35},{35,18},{19,36},{36,19},{2... | collective-permute-start | bytes 1769480 | tf_op jit(solution)/shard_map/ppermute | solution.py:23
  25.7 0.7 collective-permute-start.2
  27.7 0.0 collective-permute-done.near
  27.8 2.1 %own.1 = (f32[256,1152]{1,0:T(8,128)S(1)}, f32[256,1152]{1,0:T(8,128)S(1)}, bf16[256,1152]{1,0:T(8,128)(2,1)S(1)}, bf16[256,1152]{1,0:T(8,128)(2,1)S(1)}, f32[25...) custom-call(f32[1]{0:T(128)S(6)} %copy.10.multiplier, f32[1]{0:T(128)S(6)} %copy.11.shift, ...), custom_call_target="tpu_custom_call" | custom-call | tf_op jit(solution)/shard_map/own/pallas_call | solution.py:151
  29.9 12.4 %collective-permute-done.3.far = bf16[256,1152]{1,0:T(8,128)(2,1)S(1)} collective-permute-done((bf16[256,1152]{1,0:T(8,128)(2,1)S(1)}, bf16[256,1152]{1,0:T(8,128)(2,1)S(1)}, u32[]{:S(2)}, u32[]{:S(2)}) %collective-permute-start.3) | collective-permute-done | bytes 589856 | tf_op jit(solution)/shard_map/ppermute | solution.py:23
  42.3 0.0 collective-permute-done.4.near
  42.3 4.0 %first.1 = (f32[256,1152]{1,0:T(8,128)}, f32[256,1152]{1,0:T(8,128)}) custom-call(f32[1]{0:T(128)S(6)} %copy.10.multiplier, f32[1]{0:T(128)S(6)} %copy.11.shift, s32[1]{0:T(128)} %bitcast.odd, bf16[256,1152]{1,0:T(8,128)(2,1)S(1)} %get-tuple-element.18.first.own, f32[256,1152]{1,0:T(8,128)S(1)} %get-tuple-element.15.start, ...), custom_call_target="tpu_custom_call" | custom-call | tf_op jit(solution)/shard_map/first/pallas_call | solution.py:165
  46.3 49.1 %collective-permute-done.1.far = bf16[256,1152]{1,0:T(8,128)(2,1)S(1)} collective-permute-done((bf16[256,1152]{1,0:T(8,128)(2,1)S(1)}, bf16[256,1152]{1,0:T(8,128)(2,1)S(1)}, u32[]{:S(2)}, u32[]{:S(2)}) %collective-permute-start.1) | collective-permute-done | bytes 589856 | tf_op jit(solution)/shard_map/ppermute | solution.py:23
  95.4 0.0 collective-permute-done.2.near
  95.4 2.1 %second.1 = (f32[256,1152]{1,0:T(8,128)}, f32[256,1152]{1,0:T(8,128)}) custom-call(f32[1]{0:T(128)S(6)} %copy.10.multiplier, f32[1]{0:T(128)S(6)} %copy.11.shift, s32[1]{0:T(128)} %bitcast.odd, s32[1]{0:T(128)} %bitcast.1.late, bf16[256,1152]{1,0:T(8,128)(2,1)S(1)} %get-tuple-element.19.second.own, ...), custom_call_target="tpu_custom_call", output_to_operand_aliasing={{0}: (12, {}), {1}: (13, {})} | custom-call | tf_op jit(solution)/shard_map/second/pallas_call | solution.py:165
Async XLA Ops:
  2.0 25.7 %collective-permute-start = (bf16[256,1152]{1,0:T(8,128)(2,1)S(1)}, bf16[256,1152]{1,0:T(8,128)(2,1)S(1)}, u32[]{:S(2)}, u32[]{:S(2)}) collective-permute-start(bf16[256,1152]{1,0:T(8,128)(2,1)S(1)} %get-tuple-element.19.second.own), channel_id=1, source_target_pairs={{16,32},{32,16},{18,34},{34,18},{20,36},{36,20},{22,38},{38,22},{2... | collective-permute-start | bytes 1769480 | tf_op jit(solution)/shard_map/ppermute | solution.py:23
  7.4 34.9 %collective-permute-start.3 = (bf16[256,1152]{1,0:T(8,128)(2,1)S(1)}, bf16[256,1152]{1,0:T(8,128)(2,1)S(1)}, u32[]{:S(2)}, u32[]{:S(2)}) collective-permute-start(bf16[256,1152]{1,0:T(8,128)(2,1)S(1)} %get-tuple-element.18.first.own), channel_id=1, source_target_pairs={{0,17},{17,0},{1,18},{18,1},{2,19},{19,2},{3,20},{20,3},{4,21},{21... | collective-permute-start | bytes 1769480 | tf_op jit(solution)/shard_map/ppermute | solution.py:23
  21.9 20.4 %collective-permute-start.4 = (bf16[256,1152]{1,0:T(8,128)(2,1)S(1)}, bf16[256,1152]{1,0:T(8,128)(2,1)}, u32[]{:S(2)}, u32[]{:S(2)}) collective-permute-start(bf16[256,1152]{1,0:T(8,128)(2,1)S(1)} %get-tuple-element.18.first.own), channel_id=1, source_target_pairs={{0,16},{16,0},{1,17},{17,1},{2,18},{18,2},{3,19},{19,3},{4,20},{20... | collective-permute-start | bytes 1769480 | tf_op jit(solution)/shard_map/ppermute | solution.py:23
  23.8 71.6 %collective-permute-start.1 = (bf16[256,1152]{1,0:T(8,128)(2,1)S(1)}, bf16[256,1152]{1,0:T(8,128)(2,1)S(1)}, u32[]{:S(2)}, u32[]{:S(2)}) collective-permute-start(bf16[256,1152]{1,0:T(8,128)(2,1)S(1)} %get-tuple-element.19.second.own), channel_id=1, source_target_pairs={{16,33},{33,16},{17,34},{34,17},{18,35},{35,18},{19,36},{36,19},{2... | collective-permute-start | bytes 1769480 | tf_op jit(solution)/shard_map/ppermute | solution.py:23
  25.7 69.7 %collective-permute-start.2 = (bf16[256,1152]{1,0:T(8,128)(2,1)S(1)}, bf16[256,1152]{1,0:T(8,128)(2,1)S(1)}, u32[]{:S(2)}, u32[]{:S(2)}) collective-permute-start(bf16[256,1152]{1,0:T(8,128)(2,1)S(1)} %get-tuple-element.19.second.own), channel_id=1, source_target_pairs={{17,33},{33,17},{19,35},{35,19},{21,37},{37,21},{23,39},{39,23},{2... | collective-permute-start | bytes 1769480 | tf_op jit(solution)/shard_map/ppermute | solution.py:23

commit v4 on v3

--- a/solution.py
+++ b/solution.py
@@ -6,20 +6,18 @@
 from jax.sharding import PartitionSpec as P
 
 AXES = ("row", "col")
-FIRST = 0
 WIDTH = 256
 
 
-def swapped(block, cols_on, parity, columns=None):
+def moved(block, way):
     n_row, n_col = (lax.axis_size(a) for a in AXES)
     route = []
-    for r in range(parity, n_row, 2):
+    for r in range(n_row):
         for c in range(n_col):
-            if columns is not None and c % 2 != columns:
-                continue
-            here = r * n_col + c
-            there = (r + 1) % n_row * n_col + (c + cols_on) % n_col
-            route += [(here, there), (there, here)]
+            on = way(r, c)
+            if on is not None:
+                there = (r + on[0]) % n_row * n_col + (c + on[1]) % n_col
+                route.append((r * n_col + c, there))
     return lax.ppermute(block, AXES, route)
 
 
@@ -51,22 +49,29 @@
     return jnp.dot(weights, other_unit, preferred_element_type=jnp.float32)
 
 
-def own_kernel(multiplier, shift, first, second, near, *outs):
+def own_kernel(multiplier, shift, odd, first, second, moved_text, *outs):
     d_first, d_second, own_unit, rest, inverse_out, inner_out = outs
     first_unit = unit(first[...])
     values = second[...].astype(jnp.float32)
     inverse = inverse_norm(values)
     own_float = values * inverse
     second_unit = own_float.astype(jnp.bfloat16)
+    other_unit = unit(moved_text[...])
     d_first[...] = tile_sum(first_unit, second_unit, multiplier, shift, True)
-    grad = tile_sum(second_unit, first_unit, multiplier, shift, True) + tile_sum(
-        second_unit, unit(near[...]), multiplier, shift
-    )
-    d_second[...] = grad
+    d_second[...] = tile_sum(second_unit, first_unit, multiplier, shift, True)
+
+    @pl.when(odd[0] == 1)
+    def _():
+        d_first[...] += tile_sum(first_unit, other_unit, multiplier, shift)
+
+    @pl.when(odd[0] == 0)
+    def _():
+        d_second[...] += tile_sum(second_unit, other_unit, multiplier, shift)
+
     own_unit[...] = second_unit
     rest[...] = (own_float - second_unit.astype(jnp.float32)).astype(jnp.bfloat16)
     inverse_out[...] = jnp.broadcast_to(inverse, inverse_out.shape)
-    inner = jnp.sum(own_float * grad, axis=-1, keepdims=True)
+    inner = jnp.sum(own_float * d_second[...], axis=-1, keepdims=True)
     inner_out[...] = jnp.broadcast_to(inner, inner_out.shape)
 
 
@@ -84,20 +89,40 @@
                 getattr(copy, action)()
 
 
-def first_kernel(multiplier, shift, odd, own, start, far, near, d_images, d_texts, total, sems):
+def image_kernel(
+    multiplier, shift, odd, moved_image, first, first_start, second, second_start, second_unit,
+    second_inverse, second_inner, first_sum, second_sum, inner_out
+):
+    other_unit = unit(moved_image[...])
+
+    @pl.when(odd[0] == 0)
+    def _():
+        first_sum[...] = first_start[...] + tile_sum(
+            unit(first[...]), other_unit, multiplier, shift
+        )
+        second_sum[...] = second_start[...]
+        inner_out[...] = second_inner[...]
+
+    @pl.when(odd[0] == 1)
+    def _():
+        grad = tile_sum(second_unit[...], other_unit, multiplier, shift)
+        first_sum[...] = first_start[...]
+        second_sum[...] = second_start[...] + grad
+        second_float = second[...].astype(jnp.float32) * second_inverse[:, :1]
+        inner_out[...] = second_inner[...] + jnp.sum(second_float * grad, axis=-1, keepdims=True)
+
+
+def first_kernel(multiplier, shift, odd, own, start, near, d_images, d_texts, total, sems):
     values = own[...].astype(jnp.float32)
     inverse = inverse_norm(values)
     own_float = values * inverse
     own_unit = own_float.astype(jnp.bfloat16)
-    grad = start[...]
-    for block in (far, near):
-        grad += tile_sum(own_unit, unit(block[...]), multiplier, shift)
+    grad = start[...] + tile_sum(own_unit, unit(near[...]), multiplier, shift)
     inner = jnp.sum(own_float * grad, axis=-1, keepdims=True)
     total[...] = (grad - own_float * inner) * inverse
     parts = list(enumerate(parts_of(own.shape[1])))
-    image_side = jnp.where(odd[0] == FIRST, 0, 1)
     for action in ("start", "wait"):
-        write_out(action, parts, total, (d_texts, d_images), image_side, sems)
+        write_out(action, parts, total, (d_texts, d_images), odd[0], sems)
 
 
 def second_kernel(
@@ -113,7 +138,7 @@
         weights.astype(jnp.float32) * exact, axis=-1, keepdims=True
     )
     parts = list(enumerate(parts_of(own.shape[1])))
-    text_side = jnp.where(odd[0] == FIRST, 0, 1)
+    text_side = jnp.where(odd[0] == 0, 0, 1)
 
     def finish(begun, inner):
         inner = inner * scale
@@ -144,18 +169,30 @@
 PARAMS = pltpu.CompilerParams(vmem_limit_bytes=32 << 20)
 
 
-def own_call(multiplier, shift, first, second, near):
+def own_call(multiplier, shift, odd, first, second, moved_text):
     grad = jax.ShapeDtypeStruct(first.shape, jnp.float32)
     block = jax.ShapeDtypeStruct(first.shape, jnp.bfloat16)
     column = jax.ShapeDtypeStruct((first.shape[0], 128), jnp.float32)
     return pl.pallas_call(
         own_kernel,
         out_shape=(grad, grad, block, block, column, column),
-        in_specs=[SCALAR] * 2 + [WHOLE] * 3,
+        in_specs=[SCALAR] * 3 + [WHOLE] * 3,
         out_specs=[WHOLE] * 6,
         compiler_params=PARAMS,
         name="own",
-    )(multiplier, shift, first, second, near)
+    )(multiplier, shift, odd, first, second, moved_text)
+
+
+def image_call(multiplier, shift, odd, *blocks):
+    sums = (blocks[2], blocks[4], blocks[7])
+    return pl.pallas_call(
+        image_kernel,
+        out_shape=tuple(jax.ShapeDtypeStruct(x.shape, x.dtype) for x in sums),
+        in_specs=[SCALAR] * 3 + [WHOLE] * len(blocks),
+        out_specs=[WHOLE] * 3,
+        compiler_params=PARAMS,
+        name="image",
+    )(multiplier, shift, odd, *blocks)
 
 
 def side_call(kernel, scalars, blocks, held, scratch, name):
@@ -181,25 +218,31 @@
 def per_device(picture_embeds, caption_embeds, logit_multiplier, offset_shift):
     scalars = (logit_multiplier, offset_shift)
     odd, late = ((lax.axis_index(a) % 2).astype(jnp.int32)[None] for a in AXES)
-    first = jnp.where(odd == FIRST, caption_embeds, picture_embeds)
-    second = jnp.where(odd == FIRST, picture_embeds, caption_embeds)
-    early_near = swapped(second, 0, 1 - FIRST, 0)
-    first_far, first_near = swapped(first, 1, FIRST), swapped(first, 0, FIRST)
-    second_far = swapped(second, 1, 1 - FIRST)
-    late_near = swapped(second, 0, 1 - FIRST, 1)
-    first_start, *second_own = own_call(*scalars, first, second, early_near)
+    text_moved = moved(
+        caption_embeds, lambda r, c: (1, 1) if r % 2 == 0 else (1, 0) if c % 2 == 0 else None
+    )
+    image_moved = moved(
+        picture_embeds, lambda r, c: (-1, -1) if r % 2 else (-1, 0) if c % 2 == 0 else None
+    )
+    first = jnp.where(odd == 0, caption_embeds, picture_embeds)
+    second = jnp.where(odd == 0, picture_embeds, caption_embeds)
+    first_near = moved(first, lambda r, c: (-1, 0) if r % 2 else (1, 0))
+    second_far = moved(second, lambda r, c: (1, 1) if r % 2 else (-1, -1))
+    late_near = moved(second, lambda r, c: None if c % 2 == 0 else (1, 0) if r % 2 else (-1, 0))
+    first_start, second_start, second_unit, rest, inverse, inner = own_call(
+        *scalars, odd, first, second, text_moved
+    )
+    first_sum, second_sum, inner = image_call(
+        *scalars, odd, image_moved, first, first_start,
+        second, second_start, second_unit, inverse, inner,
+    )
     held = side_call(
-        first_kernel,
-        (*scalars, odd),
-        (first, first_start, first_far, first_near),
-        (),
-        (),
-        "first",
+        first_kernel, (*scalars, odd), (first, first_sum, first_near), (), (), "first"
     )
     return side_call(
         second_kernel,
         (*scalars, odd, late),
-        (second, *second_own, second_far, late_near),
+        (second, second_sum, second_unit, rest, inverse, inner, second_far, late_near),
         held,
         (jnp.bfloat16, jnp.float32),
         "second",

time: 99 us -> 98.6 us (level)
  waiting for transfers between devices: 61.5 us -> 52.7 us
  starting transfers between devices: 24.4 us -> 31.2 us
  Pallas kernels: 8.23 us -> 10.2 us
    ppermute x5, waiting for transfers between devices: 61.5 us -> 52.7 us  [moved(): return lax.ppermute(block, AXES, route)]
    ppermute x5, starting transfers between devices: 24.4 us -> 31.2 us  [moved(): return lax.ppermute(block, AXES, route)]
    pallas_call x0 -> x1, Pallas kernels: none -> 1.28 us  [image_call(): pl.pallas_call(image_kernel, out_shape=tuple((jax.ShapeDtypeStruct(x.shap...]
    pallas_call x1, Pallas kernels: 2.11 us -> 3.33 us  [own_call(): pl.pallas_call(own_kernel, out_shape=(grad, grad, block, block, column, c...]
  transfers between devices with their start and end apart: 5 -> 5, of which waited for: 2 -> 2; matrix products, arithmetic and copies ran while one was open for 0% -> 1% of each run, Pallas kernels for 6% -> 8%
where the time goes in v4:
time: 98.6 us; the launch traced here: 97.5 us
  waiting for transfers between devices  52.7 us (53%)
  starting transfers between devices  31.2 us (32%)
  Pallas kernels  10.2 us (10%)
  between operations  2.03 us (2%)
  other arithmetic  1.35 us (1%)
    ppermute x5, waiting for transfers between devices, moved(): return lax.ppermute(block, AXES, route)  52.7 us
    ppermute x5, starting transfers between devices, moved(): return lax.ppermute(block, AXES, route)  31.2 us
    pallas_call x2, Pallas kernels, side_call(): pl.pallas_call(kernel, out_shape=(grad, grad), in_specs=[SCALAR] * len(sc...  5.63 us
    pallas_call x1, Pallas kernels, own_call(): pl.pallas_call(own_kernel, out_shape=(grad, grad, block, block, column, c...  3.33 us
  transfers between devices with their start and end apart: 5, of which 2 were waited for; matrix products, arithmetic and copies ran while one was open for 1% of the time, Pallas kernels for 8%

profile of v4, /device:TPU:1, one launch (start us, length us, event | category | flops | bytes accessed | tf_op | source)
XLA Modules:
  0.0 97.5 jit_solution(306706630220602390)
XLA Ops:
  0.6 5.4 %collective-permute-start.1 = (bf16[256,1152]{1,0:T(8,128)(2,1)}, bf16[256,1152]{1,0:T(8,128)(2,1)S(1)}, u32[]{:S(2)}, u32[]{:S(2)}) collective-permute-start(bf16[256,1152]{1,0:T(8,128)(2,1)} %param.5), channel_id=1, source_target_pairs={{0,17},{1,18},{2,19},{3,20},{4,21},{5,22},{6,23},{7,24},{8,25},{9,... | collective-permute-start | bytes 1769480 | tf_op jit(solution)/shard_map/ppermute | solution.py:21
  6.0 15.1 %collective-permute-start = (bf16[256,1152]{1,0:T(8,128)(2,1)}, bf16[256,1152]{1,0:T(8,128)(2,1)S(1)}, u32[]{:S(2)}, u32[]{:S(2)}) collective-permute-start(bf16[256,1152]{1,0:T(8,128)(2,1)} %param.4), channel_id=1, source_target_pairs={{0,752},{2,754},{4,756},{6,758},{8,760},{10,762},{12,764},{14,766}... | collective-permute-start | bytes 1769480 | tf_op jit(solution)/shard_map/ppermute | solution.py:21
  21.1 1.4 %broadcast_select_fusion = (bf16[256,1152]{1,0:T(8,128)(2,1)S(1)}, bf16[256,1152]{1,0:T(8,128)(2,1)S(1)}) fusion(bf16[256,1152]{1,0:T(8,128)(2,1)} %param.5, bf16[256,1152]{1,0:T(8,128)(2,1)} %param.4, pred[]{:T(512)} %bitcast.2), kind=kLoop, calls=%fused_computation | loop fusion | flops 589824 | bytes 2359297 | tf_op jit(solution)/shard_map/jit(_where)/select_n | solution.py:227
  22.5 4.4 %collective-permute-start.4 = (bf16[256,1152]{1,0:T(8,128)(2,1)S(1)}, bf16[256,1152]{1,0:T(8,128)(2,1)}, u32[]{:S(2)}, u32[]{:S(2)}) collective-permute-start(bf16[256,1152]{1,0:T(8,128)(2,1)S(1)} %get-tuple-element.24.first.own), channel_id=1, source_target_pairs={{0,16},{1,17},{2,18},{3,19},{4,20},{5,21},{6,22},{7,23},{8,24},{9,... | collective-permute-start | bytes 1769480 | tf_op jit(solution)/shard_map/ppermute | solution.py:21
  26.9 5.6 %collective-permute-start.2 = (bf16[256,1152]{1,0:T(8,128)(2,1)S(1)}, bf16[256,1152]{1,0:T(8,128)(2,1)S(1)}, u32[]{:S(2)}, u32[]{:S(2)}) collective-permute-start(bf16[256,1152]{1,0:T(8,128)(2,1)S(1)} %get-tuple-element.25.second.own), channel_id=1, source_target_pairs={{0,767},{1,752},{2,753},{3,754},{4,755},{5,756},{6,757},{7,758},{8... | collective-permute-start | bytes 1769480 | tf_op jit(solution)/shard_map/ppermute | solution.py:21
  32.6 0.7 collective-permute-start.3
  34.6 0.0 collective-permute-done.1.moved_text
  34.6 3.3 %own.1 = (f32[256,1152]{1,0:T(8,128)S(1)}, f32[256,1152]{1,0:T(8,128)S(1)}, bf16[256,1152]{1,0:T(8,128)(2,1)S(1)}, bf16[256,1152]{1,0:T(8,128)(2,1)S(1)}, f32[25...) custom-call(f32[1]{0:T(128)S(6)} %copy.10.multiplier, f32[1]{0:T(128)S(6)} %copy.11.shift, s32[1]{0:T(128)} %bitcast.odd, ...), custom_call_target="tpu_custom_call" | custom-call | tf_op jit(solution)/shard_map/own/pallas_call | solution.py:176
  37.9 49.1 %collective-permute-done.moved_image = bf16[256,1152]{1,0:T(8,128)(2,1)S(1)} collective-permute-done((bf16[256,1152]{1,0:T(8,128)(2,1)}, bf16[256,1152]{1,0:T(8,128)(2,1)S(1)}, u32[]{:S(2)}, u32[]{:S(2)}) %collective-permute-start) | collective-permute-done | bytes 589856 | tf_op jit(solution)/shard_map/ppermute | solution.py:21
  87.0 1.3 %image.1 = (f32[256,1152]{1,0:T(8,128)S(1)}, f32[256,1152]{1,0:T(8,128)S(1)}, f32[256,128]{1,0:T(8,128)S(1)}) custom-call(f32[1]{0:T(128)S(6)} %copy.10.multiplier, f32[1]{0:T(128)S(6)} %copy.11.shift, s32[1]{0:T(128)} %bitcast.odd, bf16[256,1152]{1,0:T(8,128)(2,1)S(1)} %collective-permute-done.moved_image, ...), custom_call_target="tpu_custom_call" | custom-call | tf_op jit(solution)/shard_map/image/pallas_call | solution.py:188
  88.3 0.0 collective-permute-done.4.near
  88.3 3.5 %first.1 = (f32[256,1152]{1,0:T(8,128)}, f32[256,1152]{1,0:T(8,128)}) custom-call(f32[1]{0:T(128)S(6)} %copy.10.multiplier, f32[1]{0:T(128)S(6)} %copy.11.shift, s32[1]{0:T(128)} %bitcast.odd, bf16[256,1152]{1,0:T(8,128)(2,1)S(1)} %get-tuple-element.24.first.own, f32[256,1152]{1,0:T(8,128)S(1)} %get-tuple-element.21.start, ...), custom_call_target="tpu_custom_call" | custom-call | tf_op jit(solution)/shard_map/first/pallas_call | solution.py:202
  91.9 3.5 %collective-permute-done.2.far = bf16[256,1152]{1,0:T(8,128)(2,1)S(1)} collective-permute-done((bf16[256,1152]{1,0:T(8,128)(2,1)S(1)}, bf16[256,1152]{1,0:T(8,128)(2,1)S(1)}, u32[]{:S(2)}, u32[]{:S(2)}) %collective-permute-start.2) | collective-permute-done | bytes 589856 | tf_op jit(solution)/shard_map/ppermute | solution.py:21
  95.4 0.0 collective-permute-done.3.near
  95.4 2.1 %second.1 = (f32[256,1152]{1,0:T(8,128)}, f32[256,1152]{1,0:T(8,128)}) custom-call(f32[1]{0:T(128)S(6)} %copy.10.multiplier, f32[1]{0:T(128)S(6)} %copy.11.shift, s32[1]{0:T(128)} %bitcast.odd, s32[1]{0:T(128)} %bitcast.1.late, bf16[256,1152]{1,0:T(8,128)(2,1)S(1)} %get-tuple-element.25.second.own, ...), custom_call_target="tpu_custom_call", output_to_operand_aliasing={{0}: (12, {}), {1}: (13, {})} | custom-call | tf_op jit(solution)/shard_map/second/pallas_call | solution.py:202
Async XLA Ops:
  0.6 33.9 %collective-permute-start.1 = (bf16[256,1152]{1,0:T(8,128)(2,1)}, bf16[256,1152]{1,0:T(8,128)(2,1)S(1)}, u32[]{:S(2)}, u32[]{:S(2)}) collective-permute-start(bf16[256,1152]{1,0:T(8,128)(2,1)} %param.5), channel_id=1, source_target_pairs={{0,17},{1,18},{2,19},{3,20},{4,21},{5,22},{6,23},{7,24},{8,25},{9,... | collective-permute-start | bytes 1769480 | tf_op jit(solution)/shard_map/ppermute | solution.py:21
  6.0 81.0 %collective-permute-start = (bf16[256,1152]{1,0:T(8,128)(2,1)}, bf16[256,1152]{1,0:T(8,128)(2,1)S(1)}, u32[]{:S(2)}, u32[]{:S(2)}) collective-permute-start(bf16[256,1152]{1,0:T(8,128)(2,1)} %param.4), channel_id=1, source_target_pairs={{0,752},{2,754},{4,756},{6,758},{8,760},{10,762},{12,764},{14,766}... | collective-permute-start | bytes 1769480 | tf_op jit(solution)/shard_map/ppermute | solution.py:21
  22.5 65.8 %collective-permute-start.4 = (bf16[256,1152]{1,0:T(8,128)(2,1)S(1)}, bf16[256,1152]{1,0:T(8,128)(2,1)}, u32[]{:S(2)}, u32[]{:S(2)}) collective-permute-start(bf16[256,1152]{1,0:T(8,128)(2,1)S(1)} %get-tuple-element.24.first.own), channel_id=1, source_target_pairs={{0,16},{1,17},{2,18},{3,19},{4,20},{5,21},{6,22},{7,23},{8,24},{9,... | collective-permute-start | bytes 1769480 | tf_op jit(solution)/shard_map/ppermute | solution.py:21
  26.9 68.5 %collective-permute-start.2 = (bf16[256,1152]{1,0:T(8,128)(2,1)S(1)}, bf16[256,1152]{1,0:T(8,128)(2,1)S(1)}, u32[]{:S(2)}, u32[]{:S(2)}) collective-permute-start(bf16[256,1152]{1,0:T(8,128)(2,1)S(1)} %get-tuple-element.25.second.own), channel_id=1, source_target_pairs={{0,767},{1,752},{2,753},{3,754},{4,755},{5,756},{6,757},{7,758},{8... | collective-permute-start | bytes 1769480 | tf_op jit(solution)/shard_map/ppermute | solution.py:21
  32.6 62.9 %collective-permute-start.3 = (bf16[256,1152]{1,0:T(8,128)(2,1)S(1)}, bf16[256,1152]{1,0:T(8,128)(2,1)S(1)}, u32[]{:S(2)}, u32[]{:S(2)}) collective-permute-start(bf16[256,1152]{1,0:T(8,128)(2,1)S(1)} %get-tuple-element.25.second.own), channel_id=1, source_target_pairs={{1,753},{3,755},{5,757},{7,759},{9,761},{11,763},{13,765},{15,767}... | collective-permute-start | bytes 1769480 | tf_op jit(solution)/shard_map/ppermute | solution.py:21

commit v5 on v3

--- a/solution.py
+++ b/solution.py
@@ -7,7 +7,7 @@
 
 AXES = ("row", "col")
 FIRST = 0
-WIDTH = 256
+WIDTH = 128
 
 
 def swapped(block, cols_on, parity, columns=None):

time: 99 us -> 99.1 us (level)
  no operation moved by 1% of the time
where the time goes in v5:
time: 99.1 us; the launch traced here: 97.5 us
  waiting for transfers between devices  61.5 us (62%)
  starting transfers between devices  24.4 us (25%)
  Pallas kernels  8.3 us (8%)
  between operations  2.01 us (2%)
  other arithmetic  1.35 us (1%)
    ppermute x5, waiting for transfers between devices, swapped(): return lax.ppermute(block, AXES, route)  61.5 us
    ppermute x5, starting transfers between devices, swapped(): return lax.ppermute(block, AXES, route)  24.4 us
    pallas_call x2, Pallas kernels, side_call(): pl.pallas_call(kernel, out_shape=(grad, grad), in_specs=[SCALAR] * len(sc...  6.19 us
    pallas_call x1, Pallas kernels, own_call(): pl.pallas_call(own_kernel, out_shape=(grad, grad, block, block, column, c...  2.11 us
  transfers between devices with their start and end apart: 5, of which 2 were waited for; matrix products, arithmetic and copies ran while one was open for 0% of the time, Pallas kernels for 6%

profile of v5, /device:TPU:1, one launch (start us, length us, event | category | flops | bytes accessed | tf_op | source)
XLA Modules:
  0.0 97.5 jit_solution(8547493154464183115)
XLA Ops:
  0.6 1.4 %broadcast_select_fusion = (bf16[256,1152]{1,0:T(8,128)(2,1)S(1)}, bf16[256,1152]{1,0:T(8,128)(2,1)S(1)}) fusion(bf16[256,1152]{1,0:T(8,128)(2,1)} %param.5, bf16[256,1152]{1,0:T(8,128)(2,1)} %param.4, pred[]{:T(512)} %bitcast.2), kind=kLoop, calls=%fused_computation | loop fusion | flops 589824 | bytes 2359297 | tf_op jit(solution)/shard_map/jit(_where)/select_n | solution.py:184
  2.0 5.4 %collective-permute-start = (bf16[256,1152]{1,0:T(8,128)(2,1)S(1)}, bf16[256,1152]{1,0:T(8,128)(2,1)S(1)}, u32[]{:S(2)}, u32[]{:S(2)}) collective-permute-start(bf16[256,1152]{1,0:T(8,128)(2,1)S(1)} %get-tuple-element.19.second.own), channel_id=1, source_target_pairs={{16,32},{32,16},{18,34},{34,18},{20,36},{36,20},{22,38},{38,22},{2... | collective-permute-start | bytes 1769480 | tf_op jit(solution)/shard_map/ppermute | solution.py:23
  7.4 14.5 %collective-permute-start.3 = (bf16[256,1152]{1,0:T(8,128)(2,1)S(1)}, bf16[256,1152]{1,0:T(8,128)(2,1)S(1)}, u32[]{:S(2)}, u32[]{:S(2)}) collective-permute-start(bf16[256,1152]{1,0:T(8,128)(2,1)S(1)} %get-tuple-element.18.first.own), channel_id=1, source_target_pairs={{0,17},{17,0},{1,18},{18,1},{2,19},{19,2},{3,20},{20,3},{4,21},{21... | collective-permute-start | bytes 1769480 | tf_op jit(solution)/shard_map/ppermute | solution.py:23
  21.9 1.9 %collective-permute-start.4 = (bf16[256,1152]{1,0:T(8,128)(2,1)S(1)}, bf16[256,1152]{1,0:T(8,128)(2,1)}, u32[]{:S(2)}, u32[]{:S(2)}) collective-permute-start(bf16[256,1152]{1,0:T(8,128)(2,1)S(1)} %get-tuple-element.18.first.own), channel_id=1, source_target_pairs={{0,16},{16,0},{1,17},{17,1},{2,18},{18,2},{3,19},{19,3},{4,20},{20... | collective-permute-start | bytes 1769480 | tf_op jit(solution)/shard_map/ppermute | solution.py:23
  23.8 1.9 %collective-permute-start.1 = (bf16[256,1152]{1,0:T(8,128)(2,1)S(1)}, bf16[256,1152]{1,0:T(8,128)(2,1)S(1)}, u32[]{:S(2)}, u32[]{:S(2)}) collective-permute-start(bf16[256,1152]{1,0:T(8,128)(2,1)S(1)} %get-tuple-element.19.second.own), channel_id=1, source_target_pairs={{16,33},{33,16},{17,34},{34,17},{18,35},{35,18},{19,36},{36,19},{2... | collective-permute-start | bytes 1769480 | tf_op jit(solution)/shard_map/ppermute | solution.py:23
  25.7 0.7 collective-permute-start.2
  27.7 0.0 collective-permute-done.near
  27.8 2.1 %own.1 = (f32[256,1152]{1,0:T(8,128)S(1)}, f32[256,1152]{1,0:T(8,128)S(1)}, bf16[256,1152]{1,0:T(8,128)(2,1)S(1)}, bf16[256,1152]{1,0:T(8,128)(2,1)S(1)}, f32[25...) custom-call(f32[1]{0:T(128)S(6)} %copy.10.multiplier, f32[1]{0:T(128)S(6)} %copy.11.shift, ...), custom_call_target="tpu_custom_call" | custom-call | tf_op jit(solution)/shard_map/own/pallas_call | solution.py:151
  29.9 12.4 %collective-permute-done.3.far = bf16[256,1152]{1,0:T(8,128)(2,1)S(1)} collective-permute-done((bf16[256,1152]{1,0:T(8,128)(2,1)S(1)}, bf16[256,1152]{1,0:T(8,128)(2,1)S(1)}, u32[]{:S(2)}, u32[]{:S(2)}) %collective-permute-start.3) | collective-permute-done | bytes 589856 | tf_op jit(solution)/shard_map/ppermute | solution.py:23
  42.3 0.0 collective-permute-done.4.near
  42.3 4.1 %first.1 = (f32[256,1152]{1,0:T(8,128)}, f32[256,1152]{1,0:T(8,128)}) custom-call(f32[1]{0:T(128)S(6)} %copy.10.multiplier, f32[1]{0:T(128)S(6)} %copy.11.shift, s32[1]{0:T(128)} %bitcast.odd, bf16[256,1152]{1,0:T(8,128)(2,1)S(1)} %get-tuple-element.18.first.own, f32[256,1152]{1,0:T(8,128)S(1)} %get-tuple-element.15.start, ...), custom_call_target="tpu_custom_call" | custom-call | tf_op jit(solution)/shard_map/first/pallas_call | solution.py:165
  46.4 49.0 %collective-permute-done.1.far = bf16[256,1152]{1,0:T(8,128)(2,1)S(1)} collective-permute-done((bf16[256,1152]{1,0:T(8,128)(2,1)S(1)}, bf16[256,1152]{1,0:T(8,128)(2,1)S(1)}, u32[]{:S(2)}, u32[]{:S(2)}) %collective-permute-start.1) | collective-permute-done | bytes 589856 | tf_op jit(solution)/shard_map/ppermute | solution.py:23
  95.4 0.0 collective-permute-done.2.near
  95.4 2.1 %second.1 = (f32[256,1152]{1,0:T(8,128)}, f32[256,1152]{1,0:T(8,128)}) custom-call(f32[1]{0:T(128)S(6)} %copy.10.multiplier, f32[1]{0:T(128)S(6)} %copy.11.shift, s32[1]{0:T(128)} %bitcast.odd, s32[1]{0:T(128)} %bitcast.1.late, bf16[256,1152]{1,0:T(8,128)(2,1)S(1)} %get-tuple-element.19.second.own, ...), custom_call_target="tpu_custom_call", output_to_operand_aliasing={{0}: (12, {}), {1}: (13, {})} | custom-call | tf_op jit(solution)/shard_map/second/pallas_call | solution.py:165
Async XLA Ops:
  2.0 25.7 %collective-permute-start = (bf16[256,1152]{1,0:T(8,128)(2,1)S(1)}, bf16[256,1152]{1,0:T(8,128)(2,1)S(1)}, u32[]{:S(2)}, u32[]{:S(2)}) collective-permute-start(bf16[256,1152]{1,0:T(8,128)(2,1)S(1)} %get-tuple-element.19.second.own), channel_id=1, source_target_pairs={{16,32},{32,16},{18,34},{34,18},{20,36},{36,20},{22,38},{38,22},{2... | collective-permute-start | bytes 1769480 | tf_op jit(solution)/shard_map/ppermute | solution.py:23
  7.4 34.9 %collective-permute-start.3 = (bf16[256,1152]{1,0:T(8,128)(2,1)S(1)}, bf16[256,1152]{1,0:T(8,128)(2,1)S(1)}, u32[]{:S(2)}, u32[]{:S(2)}) collective-permute-start(bf16[256,1152]{1,0:T(8,128)(2,1)S(1)} %get-tuple-element.18.first.own), channel_id=1, source_target_pairs={{0,17},{17,0},{1,18},{18,1},{2,19},{19,2},{3,20},{20,3},{4,21},{21... | collective-permute-start | bytes 1769480 | tf_op jit(solution)/shard_map/ppermute | solution.py:23
  21.9 20.4 %collective-permute-start.4 = (bf16[256,1152]{1,0:T(8,128)(2,1)S(1)}, bf16[256,1152]{1,0:T(8,128)(2,1)}, u32[]{:S(2)}, u32[]{:S(2)}) collective-permute-start(bf16[256,1152]{1,0:T(8,128)(2,1)S(1)} %get-tuple-element.18.first.own), channel_id=1, source_target_pairs={{0,16},{16,0},{1,17},{17,1},{2,18},{18,2},{3,19},{19,3},{4,20},{20... | collective-permute-start | bytes 1769480 | tf_op jit(solution)/shard_map/ppermute | solution.py:23
  23.8 71.6 %collective-permute-start.1 = (bf16[256,1152]{1,0:T(8,128)(2,1)S(1)}, bf16[256,1152]{1,0:T(8,128)(2,1)S(1)}, u32[]{:S(2)}, u32[]{:S(2)}) collective-permute-start(bf16[256,1152]{1,0:T(8,128)(2,1)S(1)} %get-tuple-element.19.second.own), channel_id=1, source_target_pairs={{16,33},{33,16},{17,34},{34,17},{18,35},{35,18},{19,36},{36,19},{2... | collective-permute-start | bytes 1769480 | tf_op jit(solution)/shard_map/ppermute | solution.py:23
  25.7 69.7 %collective-permute-start.2 = (bf16[256,1152]{1,0:T(8,128)(2,1)S(1)}, bf16[256,1152]{1,0:T(8,128)(2,1)S(1)}, u32[]{:S(2)}, u32[]{:S(2)}) collective-permute-start(bf16[256,1152]{1,0:T(8,128)(2,1)S(1)} %get-tuple-element.19.second.own), channel_id=1, source_target_pairs={{17,33},{33,17},{19,35},{35,19},{21,37},{37,21},{23,39},{39,23},{2... | collective-permute-start | bytes 1769480 | tf_op jit(solution)/shard_map/ppermute | solution.py:23
